TPU v7x, 32 devices: a whole 2x2x4 slice. The times are simulated.
32 devices in a mesh: rep: 4 (over x, core), tp: 8 (over z, y).
Axes of the slice: x: 2, y: 2, z: 4, core: 2. Of those that a mesh axis runs over, the one named last changes fastest.
Arguments:
- activations: bfloat16 [4, 256, 2560], P('rep', 'tp'), may hold values from -6 to 6
- out_grad: bfloat16 [4, 256, 2560], P('rep', 'tp'), may hold values from -6 to 6
- gate_weight: bfloat16 [4, 2560, 6912], P('rep', None, 'tp'), may hold values from -6 to 6
- up_weight: bfloat16 [4, 2560, 6912], P('rep', None, 'tp'), may hold values from -6 to 6
- down_weight: bfloat16 [4, 6912, 2560], P('rep', 'tp'), may hold values from -6 to 6
- step_index: int32 [1], replicated, may hold values from 0 to 999
Outputs:
- layer_out: bfloat16 [4, 256, 2560], P('rep', 'tp')
- grad_in: bfloat16 [4, 256, 2560], P('rep', 'tp')
- new_gate: bfloat16 [4, 2560, 6912], P('rep', None, 'tp')
- new_up: bfloat16 [4, 2560, 6912], P('rep', None, 'tp')
- new_down: bfloat16 [4, 6912, 2560], P('rep', 'tp')
All inputs are finite; a program needn't handle non-finite values.
Results may differ from a plain program's by a relative error of at most 0.0052.
Values may be sent and summed in bfloat16 or wider, within the bound.
No kernel may reach another device: no remote copies, remote signals or barrier semaphores. Data moves between devices by JAX's collectives and lax.ppermute only.
A program may use at most 128 MiB of HBM per device.

v0:
```python
from functools import partial
import math

import jax
import jax.numpy as jnp
from jax import lax
from jax.experimental import pallas as pl
from jax.experimental.pallas import tpu as pltpu
from jax.sharding import PartitionSpec as P

D = 2560
FF = 6912
BLOCK = 144


learn_rate = 0.8
width_scale = 1.0 / math.sqrt(D)
hidden_scale = 1.0 / math.sqrt(FF)

ANY = pl.BlockSpec(memory_space=pl.ANY)
PARAMS = pltpu.CompilerParams(vmem_limit_bytes=40 * 1024 * 1024)


def ring_of(devices):
    y_size = 1 << ((devices.bit_length() - 1) // 2)
    z_size = devices // y_size
    walk = [(z, 0) for z in range(z_size)]
    for z in reversed(range(z_size)):
        ys = list(range(1, y_size))
        walk += [(z, y) for y in (ys if (z_size - 1 - z) % 2 == 0 else reversed(ys))]
    return [z * y_size + y for z, y in walk]


def mm(a, b, dims):
    return lax.dot_general(a, b, (dims, ((), ())), preferred_element_type=jnp.float32)


def cost(matmuls, rows, blocks_moved):
    return pl.CostEstimate(
        flops=2 * matmuls * rows * 256 * D, bytes_accessed=blocks_moved * rows * D * 2, transcendentals=0
    )


def rows_spec(first=0, width=D, block=BLOCK):
    return pl.BlockSpec((block, width), lambda i: (i + first, 0))


def block_of(units, most):
    return max(size for size in range(BLOCK, most + 1, BLOCK) if units % size == 0)


def whole_spec(x):
    return pl.BlockSpec(x.shape, lambda i: (0,) * x.ndim)


def forward(token_blocks, grad_blocks, gate_w, up_w, down_w):
    units, devices = gate_w.shape[0], len(token_blocks)
    part = token_blocks[0].shape[0]
    count = devices * part
    block = block_of(units, 288)

    def body(*refs):
        gate_ref, up_ref, down_ref = refs[2 * devices : 2 * devices + 3]
        tokens_ref, grads_ref, hidden_ref, d_gate_ref, d_up_ref, turned, turned_grads = refs[-7:]

        @pl.when(pl.program_id(0) == 0)
        def _():
            for at in range(devices):
                tokens_ref[pl.ds(at * part, part)] = refs[at][...]
                grads_ref[pl.ds(at * part, part)] = refs[devices + at][...]
            turned[...] = tokens_ref[...].T
            turned_grads[...] = grads_ref[...].T

        gate_pre = mm(gate_ref[...], turned[...], ((1,), (0,))) * width_scale
        up_pre = mm(up_ref[...], turned[...], ((1,), (0,))) * width_scale
        d_hidden = mm(down_ref[...], turned_grads[...], ((1,), (0,))) * hidden_scale
        sigmoid_gate = jax.nn.sigmoid(gate_pre)
        activated = gate_pre * sigmoid_gate
        slope = sigmoid_gate * (1.0 + gate_pre * (1.0 - sigmoid_gate))
        hidden_ref[...] = (activated * up_pre).astype(jnp.bfloat16)
        d_gate_ref[...] = (d_hidden * up_pre * slope).astype(jnp.bfloat16)
        d_up_ref[...] = (d_hidden * activated).astype(jnp.bfloat16)

    whole = jax.ShapeDtypeStruct((count, D), jnp.bfloat16)
    out = jax.ShapeDtypeStruct((units, count), jnp.bfloat16)
    pieces = [*token_blocks, *grad_blocks]
    return pl.pallas_call(
        body,
        grid=(units // block,),
        in_specs=[whole_spec(piece) for piece in pieces] + [rows_spec(block=block)] * 3,
        out_specs=[whole_spec(whole)] * 2 + [rows_spec(0, count, block)] * 3,
        out_shape=[whole] * 2 + [out] * 3,
        scratch_shapes=[pltpu.VMEM((D, count), jnp.bfloat16)] * 2,
        compiler_params=PARAMS,
        cost_estimate=cost(3, units, 3),
        name="forward",
    )(*pieces, gate_w, up_w, down_w)


def stepped(weight, left, right, scale):
    return weight.astype(jnp.float32) - learn_rate * (mm(left, right, ((1,), (0,))) * scale)


def step_rows(weight, left, right, scale, first, rows, after=(), beside=None, below=None, costs=None):
    at, steps = first // BLOCK, rows // BLOCK
    count = left.shape[1]
    here = lambda i: (jnp.minimum(i, steps - 1) + at, 0)
    ins = (weight, left, right)
    specs = [pl.BlockSpec((BLOCK, D), here), pl.BlockSpec((BLOCK, count), here), whole_spec(right)]
    out_rows, width = rows, D
    if beside is not None:
        ins = (*ins, beside, below)
        specs += [pl.BlockSpec((BLOCK, count), lambda i: (jnp.minimum(i, steps - 1), 0)), whole_spec(below)]
        out_rows, width = rows + below.shape[0], D + count

    def body(weight_ref, left_ref, right_ref, *rest):
        out_ref = rest[-1]

        @pl.when(pl.program_id(0) < steps)
        def _():
            out_ref[:, :D] = stepped(weight_ref[...], left_ref[...], right_ref[...], scale).astype(jnp.bfloat16)
            if beside is not None:
                out_ref[:, D:] = rest[0][...]

        if below is not None:

            @pl.when(pl.program_id(0) == steps)
            def _():
                out_ref[pl.ds(0, below.shape[0]), :D] = rest[1][...]

    return pl.pallas_call(
        body,
        grid=(steps if below is None else steps + 1,),
        in_specs=specs + [ANY] * len(after),
        out_specs=rows_spec(0, width),
        out_shape=jax.ShapeDtypeStruct((out_rows, width), jnp.bfloat16),
        compiler_params=PARAMS,
        cost_estimate=costs or cost(1, rows, 2),
        name="step_rows",
    )(*ins, *after)


def rows_of(x, first, rows, block):
    at = first // block

    def body(x_ref, out_ref):
        out_ref[...] = x_ref[...]

    return pl.pallas_call(
        body,
        grid=(rows // block,),
        in_specs=[rows_spec(at, block=block)],
        out_specs=rows_spec(block=block),
        out_shape=jax.ShapeDtypeStruct((rows, D), x.dtype),
        compiler_params=PARAMS,
        cost_estimate=cost(0, rows, 2),
        name="rows_of",
    )(x)


def halved_sum(mine, theirs):
    return ((mine.astype(jnp.float32) + theirs.astype(jnp.float32)) * 0.5).astype(jnp.bfloat16)


def into_rows(body, ins, in_specs, base, first, rows, units, costs, name, after, scratch=()):
    others = after if base is None else (base, *after)

    def with_others(*refs):
        body(*refs[: len(ins)], *refs[len(ins) + len(others) :])
    return pl.pallas_call(
        with_others,
        grid=(rows // BLOCK,),
        in_specs=in_specs + [ANY] * len(others),
        out_specs=rows_spec(first // BLOCK),
        out_shape=jax.ShapeDtypeStruct((units, D), jnp.bfloat16),
        input_output_aliases={} if base is None else {len(ins): 0},
        scratch_shapes=scratch,
        compiler_params=PARAMS,
        cost_estimate=costs,
        name=name,
    )(*ins, *others)


def mean_rows(mine, theirs, rows, base, first, units, after=()):
    def body(mine_ref, theirs_ref, out_ref):
        out_ref[...] = halved_sum(mine_ref[...], theirs_ref[...])

    specs = [rows_spec()] * 2
    return into_rows(
        body, (mine, theirs), specs, base, first, rows, units, cost(0, rows, 3), "mean_rows", after
    )


def mean_of_steps(mine, left, right, theirs, their_left, their_blocks, scale, rows, units, after):
    part = their_blocks[0].shape[0]

    def body(mine_ref, left_ref, right_ref, theirs_ref, their_left_ref, *rest):
        out_ref, their_right = rest[-2:]

        @pl.when(pl.program_id(0) == 0)
        def _():
            for at in range(len(their_blocks)):
                their_right[pl.ds(at * part, part)] = rest[at][...]

        own = stepped(mine_ref[...], left_ref[...], right_ref[...], scale).astype(jnp.bfloat16)
        other = stepped(theirs_ref[...], their_left_ref[...], their_right[...], scale).astype(jnp.bfloat16)
        out_ref[...] = halved_sum(own, other)

    count = left.shape[1]
    return into_rows(
        body,
        (mine, left, right, theirs, their_left, *their_blocks),
        [rows_spec(), rows_spec(0, count), whole_spec(right)]
        + [rows_spec(), pl.BlockSpec((BLOCK, count), lambda i: (i, D // count))]
        + [whole_spec(block) for block in their_blocks],
        None,
        0,
        rows,
        units,
        cost(2, rows, 3),
        "mean_of_steps",
        after,
        [pltpu.VMEM((count, D), jnp.bfloat16)],
    )


def partial_sums(hidden, d_gate, d_up, gate_w, up_w, down_w, after):
    units, count = hidden.shape
    block = block_of(units, 432)
    steps = units // block

    def body(hidden_ref, d_gate_ref, d_up_ref, gate_ref, up_ref, down_ref, *rest):
        layer_ref, grad_ref = rest[-2:]

        @pl.when(pl.program_id(0) == 0)
        def _():
            layer_ref[...] = jnp.zeros_like(layer_ref)
            grad_ref[...] = jnp.zeros_like(grad_ref)

        layer_ref[...] += mm(hidden_ref[...], down_ref[...], ((0,), (0,))) * hidden_scale
        grad_sum = mm(d_gate_ref[...], gate_ref[...], ((0,), (0,))) + mm(d_up_ref[...], up_ref[...], ((0,), (0,)))
        grad_ref[...] += grad_sum * width_scale

    out = jax.ShapeDtypeStruct((count, D), jnp.float32)
    return pl.pallas_call(
        body,
        grid=(steps,),
        in_specs=[rows_spec(0, count, block)] * 3 + [rows_spec(block=block)] * 3 + [ANY] * len(after),
        out_specs=[whole_spec(out)] * 2,
        out_shape=[out] * 2,
        compiler_params=PARAMS,
        cost_estimate=cost(3, units, 3),
        name="partial_sums",
    )(hidden, d_gate, d_up, gate_w, up_w, down_w, *after)


def whole_step(distance, turned, tokens_local, grads_local, gate_w, up_w, down_w):
    units = gate_w.shape[0]
    devices = lax.axis_size("tp")
    ring = ring_of(devices)

    def send(x):
        replicas = lax.axis_size("rep")
        return lax.ppermute(x, "rep", [(i, (i + distance) % replicas) for i in range(replicas)])

    def along(x, by):
        return lax.ppermute(x, "tp", [(ring[i], ring[(i + by) % devices]) for i in range(devices)])

    blocks = units // BLOCK
    raw = (blocks if distance == 1 else blocks // 2) * BLOCK
    theirs_raw = send(up_w if raw == units else rows_of(up_w, 0, raw, BLOCK))

    half = devices // 2

    def gather(turn, locals_):
        held = [[x] * devices for x in locals_]
        for hop in range(1, half + 1):
            for at, blocks_held in enumerate(held):
                last_way = turn if at % 2 == 0 else -turn
                for way in (turn, -turn):
                    if hop < half or way == last_way:
                        blocks_held[-way * hop] = along(blocks_held[-way * (hop - 1)], way)
        return [blocks_held[1:] for blocks_held in held]

    def gathered(*locals_):
        if devices > 8:
            return [list(lax.all_gather(x, "tp")) for x in locals_]
        others = lax.cond(turned, partial(gather, 1), partial(gather, -1), locals_)
        return [[x, *rest] for x, rest in zip(locals_, others)]

    def gathered_beside(x, mine, theirs):
        if devices > 8:
            return list(lax.all_gather(x, "tp")), mean_rows(mine, theirs, units, None, 0, units)

        def branch(turn, x, mine, theirs):
            (others,) = gather(turn, (x,))
            return others, mean_rows(mine, theirs, units, None, 0, units)

        others, mean = lax.cond(turned, partial(branch, 1), partial(branch, -1), x, mine, theirs)
        return [x, *others], mean

    def summed(terms):
        if devices > 8:
            totals = [lax.psum_scatter(term, "tp", scatter_dimension=0, tiled=True) for term in terms]
            return [total.astype(jnp.bfloat16) for total in totals]
        return lax.cond(turned, partial(sums, 1), partial(sums, -1), terms)

    def sums(turn, terms):
        part = terms[0].shape[0] // devices
        block_at = lambda term, offset: term[(offset % devices) * part : (offset % devices + 1) * part]
        ways = [(at, way, half - (0 if (way == turn) == (at == 0) else 1)) for at in (0, 1) for way in (turn, -turn)]
        moving = {}
        for hop in range(1, half + 1):
            for at, way, hops in ways:
                if hop <= hops:
                    block = block_at(terms[at], way * (hops + 1 - hop))
                    if hop > 1:
                        block = block + moving[at, way].astype(jnp.float32)
                    moving[at, way] = along(block.astype(jnp.bfloat16), way)
        totals = []
        for at, term in enumerate(terms):
            total = block_at(term, 0)
            for way in (turn, -turn):
                total = total + moving[at, way].astype(jnp.float32)
            totals.append(total.astype(jnp.bfloat16))
        return totals

    token_blocks, grad_blocks = gathered(tokens_local, grads_local)
    tokens, grads, hidden, d_gate, d_up = forward(token_blocks, grad_blocks, gate_w, up_w, down_w)
    cut = units - BLOCK
    down_step = partial(step_rows, down_w, hidden, grads, hidden_scale, 0, units)
    head_step = partial(step_rows, gate_w, d_gate, tokens, width_scale, 0, cut)
    long_step = cost(20, units, 40)
    if raw < units:
        first = step_rows(
            up_w, d_up, tokens, width_scale, raw, units - raw, beside=d_up, below=tokens_local
        )
        their_first = send(first)
        second = down_new = down_step((theirs_raw,), costs=long_step)
        their_down = send(down_new)
    else:
        first = down_new = down_step(beside=d_up, below=tokens_local)
        their_first = their_down = send(down_new)
        second = gate_head = head_step((theirs_raw,), costs=long_step)
        their_gate_head = send(gate_head)
    terms = partial_sums(hidden, d_gate, d_up, gate_w, up_w, down_w, (second,))
    layer_out, grad_in = summed(terms)
    if raw < units:
        gate_head = head_step((their_first, layer_out))
        their_gate_head = send(gate_head)
    gate_tail = step_rows(gate_w, d_gate, tokens, width_scale, cut, BLOCK, (their_down, layer_out))
    their_gate_tail = send(gate_tail)

    their_tokens = rows_of(their_first, units - raw if raw < units else units, tokens_local.shape[0], 16)
    their_tokens, gate_tail = lax.optimization_barrier((their_tokens, gate_tail))
    their_blocks, new_down = gathered_beside(their_tokens, down_new, their_down)
    new_up = mean_of_steps(
        up_w, d_up, tokens, theirs_raw, their_first, their_blocks, width_scale, raw, units, (gate_tail,)
    )
    if raw < units:
        new_up = mean_rows(first, their_first, units - raw, new_up, raw, units)
    new_gate = mean_rows(gate_head, their_gate_head, cut, None, 0, units, (new_up, new_down))
    new_gate = mean_rows(gate_tail, their_gate_tail, BLOCK, new_gate, cut, units)
    return layer_out, grad_in, new_gate, new_up, new_down


def shards(activations, out_grad, gate_weight, up_weight, down_weight, step_index):
    levels = lax.axis_size("rep").bit_length() - 1
    branches = [partial(whole_step, 1 << level) for level in range(levels)]
    layer_out, grad_in, gate, up, down = lax.switch(
        step_index[0] % levels,
        branches,
        (step_index[0] // levels) % 2 == 0,
        activations[0],
        out_grad[0],
        gate_weight[0].T,
        up_weight[0].T,
        down_weight[0],
    )
    return layer_out[None], grad_in[None], gate.T[None], up.T[None], down[None]


def solution(mesh):
    in_specs = (
        P("rep", "tp", None),
        P("rep", "tp", None),
        P("rep", None, "tp"),
        P("rep", None, "tp"),
        P("rep", "tp", None),
        P(),
    )
    out_specs = (
        P("rep", "tp", None),
        P("rep", "tp", None),
        P("rep", None, "tp"),
        P("rep", None, "tp"),
        P("rep", "tp", None),
    )
    return jax.shard_map(shards, mesh=mesh, in_specs=in_specs, out_specs=out_specs, check_vma=False)
```

profile of v0, /device:TPU:0, one launch (start us, length us, event | category | flops | bytes accessed | tf_op | source)
XLA Modules:
  0.0 305.4 jit_solution(11816138123566589987)
XLA Ops:
  1.3 303.5 %conditional.21 = (bf16[32,2560]{1,0:T(8,128)(2,1)S(1)}, bf16[32,2560]{1,0:T(8,128)(2,1)}, bf16[864,2560]{1,0:T(8,128)(2,1)}, bf16[864,2560]{1,0:T(8,128)(2,1)}, bf16[864,2560]{1,0:T(8,128)(2,1)}) conditional(s32[]{:T(128)} %clamp.3, (pred[]{:T(512)}, bf16[32,2560]{1,0:T(8,128)(2,1)}, bf16[32,2560]{1,0:T(8,128)(2,1)}, bf16[864,2560]{1,0:T(8,128)(2,1)}, ...), branch_computations={%region_0.7_spmd, %region_7.14_spmd} | conditional | flops 33034731520 | bytes 460360000 | solution.py:370
  1.6 3.8 %rows_of.4 = bf16[432,2560]{1,0:T(8,128)(2,1)} custom-call(bf16[864,2560]{1,0:T(8,128)(2,1)} %get-tuple-element.187.refs_17_.x_ref.up_ref.weight_ref.refs_0_), custom_call_target="tpu_custom_call" | custom-call | bytes 4423680 | tf_op jit(solution)/shard_map/cond/branch_1_fun/rows_of/pallas_call | solution.py:149
  5.4 2.9 collective-permute-start.144
  8.4 29.3 %conditional.12 = (bf16[32,2560]{1,0:T(8,128)(2,1)}, bf16[32,2560]{1,0:T(8,128)(2,1)}, bf16[32,2560]{1,0:T(8,128)(2,1)}, bf16[32,2560]{1,0:T(8,128)(2,1)}, bf16[...) conditional(s32[]{:T(128)} %convert_element_type.361, ...), branch_computations={%region_8.8_spmd, %region_9.9_spmd} | conditional | bytes 9175712 | solution.py:288
  8.4 1.5 collective-permute-start.42
  10.4 1.6 collective-permute-start.46
  12.4 2.4 collective-permute-done.42
  14.8 2.3 collective-permute-start.43
  17.6 3.0 collective-permute-done.46
  21.1 1.5 collective-permute-start.50
  22.7 1.6 collective-permute-start.44
  24.9 3.2 %collective-permute-done.47 = bf16[32,2560]{1,0:T(8,128)(2,1)} collective-permute-done((bf16[32,2560]{1,0:T(8,128)(2,1)}, bf16[32,2560]{1,0:T(8,128)(2,1)}, u32[]{:S(2)}, u32[]{:S(2)}) %collective-permute-start.47) | collective-permute-done | bytes 163872 | tf_op jit(solution)/shard_map/cond/branch_1_fun/cond/branch_0_fun/ppermute | solution.py:267
  28.5 1.6 collective-permute-start.51
  30.1 1.6 collective-permute-start.45
  32.3 2.3 collective-permute-done.48
  35.9 1.8 collective-permute-done.55
  37.7 9.2 %forward.3 = (bf16[256,2560]{1,0:T(8,128)(2,1)S(1)}, bf16[256,2560]{1,0:T(8,128)(2,1)S(1)}, bf16[864,256]{1,0:T(8,128)(2,1)S(1)}, bf16[864,256]{1,0:T(8,128)(2,1)S(1)}, bf16[864,256]{1,0:T(8,128)(2,1)S(1)}) custom-call(bf16[32,2560]{1,0:T(8,128)(2,1)S(1)} %copy-done.12, bf16[32,2560]{1,0:T(8,128)(2,1)} %get-tuple-element.172.refs_1_, ...), custom_call_target="tpu_custom_call" | custom-call | flops 3397386240 | bytes 13271040 | tf_op jit(solution)/shard_map/cond/branch_1_fun/forward/pallas_call | solution.py:87
  47.0 2.7 step_rows.11.refs_0_
  50.2 7.4 %collective-permute-done.144.rest_0_.refs_3_ = bf16[432,2560]{1,0:T(8,128)(2,1)} collective-permute-done((bf16[432,2560]{1,0:T(8,128)(2,1)}, bf16[432,2560]{1,0:T(8,128)(2,1)}, u32[]{:S(2)}, u32[]{:S(2)}) %collective-permute-start.144) | collective-permute-done | bytes 2211872 | tf_op jit(solution)/shard_map/cond/branch_1_fun/ppermute | solution.py:264
  57.6 4.2 %step_rows.10.rest_0_ = bf16[864,2560]{1,0:T(8,128)(2,1)} custom-call(bf16[864,2560]{1,0:T(8,128)(2,1)S(1)} %copy-done.6, bf16[864,256]{1,0:T(8,128)(2,1)S(1)} %get-tuple-element.189.left_ref.hidden_ref, bf16[256,2560]{1,0:T(8,128)(2,1)S(1)} %get-tuple-element.192.right_ref, bf16[432,2560]{1,0:T(8,128)(2,1)} %collective-permute-done.144.rest_0_.refs_3_), custom_call_target="tpu_custom_call" | custom-call | flops 22649241600 | bytes 176947200 | tf_op jit(solution)/shard_map/cond/branch_1_fun/step_rows/pallas_call | solution.py:131
  61.8 6.3 %partial_sums.3 = (f32[256,2560]{1,0:T(8,128)S(1)}, f32[256,2560]{1,0:T(8,128)}) custom-call(bf16[864,256]{1,0:T(8,128)(2,1)S(1)} %get-tuple-element.189.left_ref.hidden_ref, bf16[864,256]{1,0:T(8,128)(2,1)S(1)} %get-tuple-element.190.d_gate_ref.left_ref, bf16[864,256]{1,0:T(8,128)(2,1)S(1)} %get-tuple-element.191.d_up_ref.left_ref.rest_0_.refs_1_, ...), custom_call_target="tpu_custom_call" | custom-call | flops 3397386240 | bytes 13271040 | tf_op jit(solution)/shard_map/cond/branch_1_fun/partial_sums/pallas_call | solution.py:245
  68.1 38.2 %conditional.23 = (bf16[32,2560]{1,0:T(8,128)(2,1)S(1)}, bf16[32,2560]{1,0:T(8,128)(2,1)}) conditional(s32[]{:T(128)} %convert_element_type.361, (f32[256,2560]{1,0:T(8,128)S(1)}, f32[256,2560]{1,0:T(8,128)}) %partial_sums.3, (f32[256,2560]{1,0:T(8,128)S(1)}, f32[256,2560]{1,0:T(8,128)}) %partial_sums.3), branch_computations={%region_10.10_spmd, %region_11.11_spmd} | conditional | flops 4587520 | bytes 37028444
  68.2 1.9 convert.29
  70.1 2.1 collective-permute-start.123
  72.5 2.0 collective-permute-start.116
  74.6 2.5 collective-permute-done.123
  77.1 1.5 collective-permute-start.124
  78.6 2.0 collective-permute-done.116
  80.6 1.5 collective-permute-start.117
  82.1 1.4 collective-permute-done.124
  83.6 1.5 collective-permute-start.127
  85.9 1.8 collective-permute-done.117
  87.8 1.6 collective-permute-start.118
  90.2 1.6 collective-permute-start.128
  91.8 1.7 collective-permute-done.118
  93.5 1.5 collective-permute-start.121
  95.9 1.5 collective-permute-done.128
  97.4 1.5 collective-permute-start.129
  99.0 1.6 collective-permute-done.121
  103.5 2.5 collective-permute-done.122
  106.4 1.6 collective-permute-start.146
  107.9 5.5 %collective-permute-done.145.x_ref.rest_0_.refs_4_.refs_1_ = bf16[464,2816]{1,0:T(8,128)(2,1)S(1)} collective-permute-done((bf16[464,2816]{1,0:T(8,128)(2,1)}, bf16[464,2816]{1,0:T(8,128)(2,1)S(1)}, u32[]{:S(2)}, u32[]{:S(2)}) %collective-permute-start.145) | collective-permute-done | bytes 2613280 | tf_op jit(solution)/shard_map/cond/branch_1_fun/ppermute | solution.py:264
  113.5 1.3 copy-done.1
  114.8 6.3 %step_rows.13.refs_0_ = bf16[720,2560]{1,0:T(8,128)(2,1)} custom-call(bf16[864,2560]{1,0:T(8,128)(2,1)} %get-tuple-element.186.refs_16_.gate_ref.weight_ref, bf16[864,256]{1,0:T(8,128)(2,1)S(1)} %get-tuple-element.190.d_gate_ref.left_ref, bf16[256,2560]{1,0:T(8,128)(2,1)S(1)} %copy-done.1, ...), custom_call_target="tpu_custom_call" | custom-call | flops 943718400 | bytes 7372800 | tf_op jit(solution)/shard_map/cond/branch_1_fun/step_rows/pallas_call | solution.py:131
  121.1 2.0 collective-permute-start.148
  123.1 85.1 %collective-permute-done.146.rest_0_ = bf16[864,2560]{1,0:T(8,128)(2,1)S(1)} collective-permute-done((bf16[864,2560]{1,0:T(8,128)(2,1)}, bf16[864,2560]{1,0:T(8,128)(2,1)S(1)}, u32[]{:S(2)}, u32[]{:S(2)}) %collective-permute-start.146) | collective-permute-done | bytes 4423712 | tf_op jit(solution)/shard_map/cond/branch_1_fun/ppermute | solution.py:264
  208.3 2.4 step_rows.12.refs_13_.refs_0_
  210.7 2.1 collective-permute-start.147
  212.8 25.4 %conditional.14 = (bf16[32,2560]{1,0:T(8,128)(2,1)}, bf16[32,2560]{1,0:T(8,128)(2,1)}, bf16[32,2560]{1,0:T(8,128)(2,1)}, bf16[32,2560]{1,0:T(8,128)(2,1)}, bf16[...) conditional(s32[]{:T(128)} %convert_element_type.361, ...), branch_computations={%region_12.12_spmd, %region_13.13_spmd} | conditional | bytes 17858904 | solution.py:299
  212.8 1.6 collective-permute-start.70
  214.9 3.8 %collective-permute-done.70 = bf16[32,2560]{1,0:T(8,128)(2,1)} collective-permute-done((bf16[32,2560]{1,0:T(8,128)(2,1)S(1)}, bf16[32,2560]{1,0:T(8,128)(2,1)}, u32[]{:S(2)}, u32[]{:S(2)}) %collective-permute-start.70) | collective-permute-done | bytes 163872 | tf_op jit(solution)/shard_map/cond/branch_1_fun/cond/branch_0_fun/ppermute | solution.py:267
  218.7 1.5 collective-permute-start.71
  221.0 4.6 %collective-permute-done.71 = bf16[32,2560]{1,0:T(8,128)(2,1)} collective-permute-done((bf16[32,2560]{1,0:T(8,128)(2,1)}, bf16[32,2560]{1,0:T(8,128)(2,1)}, u32[]{:S(2)}, u32[]{:S(2)}) %collective-permute-start.71) | collective-permute-done | bytes 163872 | tf_op jit(solution)/shard_map/cond/branch_1_fun/cond/branch_0_fun/ppermute | solution.py:267
  225.6 1.5 collective-permute-start.72
  228.2 4.4 %collective-permute-done.72 = bf16[32,2560]{1,0:T(8,128)(2,1)} collective-permute-done((bf16[32,2560]{1,0:T(8,128)(2,1)}, bf16[32,2560]{1,0:T(8,128)(2,1)}, u32[]{:S(2)}, u32[]{:S(2)}) %collective-permute-start.72) | collective-permute-done | bytes 163872 | tf_op jit(solution)/shard_map/cond/branch_1_fun/cond/branch_0_fun/ppermute | solution.py:267
  232.6 1.5 collective-permute-start.73
  234.1 3.5 %mean_rows.13 = bf16[864,2560]{1,0:T(8,128)(2,1)} custom-call(bf16[864,2560]{1,0:T(8,128)(2,1)S(1)} %get-tuple-element.164.refs_0_, bf16[864,2560]{1,0:T(8,128)(2,1)S(1)} %get-tuple-element.165.refs_1_), custom_call_target="tpu_custom_call" | custom-call | bytes 13271040 | tf_op jit(solution)/shard_map/cond/branch_1_fun/cond/branch_0_fun/mean_rows/pallas_call | solution.py:170
  238.3 1.3 copy-done.2
  239.6 5.0 %mean_of_steps.3.refs_2_ = bf16[864,2560]{1,0:T(8,128)(2,1)S(1)} custom-call(bf16[864,2560]{1,0:T(8,128)(2,1)} %get-tuple-element.187.refs_17_.x_ref.up_ref.weight_ref.refs_0_, bf16[864,256]{1,0:T(8,128)(2,1)S(1)} %get-tuple-element.191.d_up_ref.left_ref.rest_0_.refs_1_, bf16[256,2560]{1,0:T(8,128)(2,1)S(1)} %copy-done.2, ...), custom_call_target="tpu_custom_call" | custom-call | flops 1132462080 | bytes 6635520 | tf_op jit(solution)/shard_map/cond/branch_1_fun/mean_of_steps/pallas_call | solution.py:170
  244.6 2.7 mean_rows.15.refs_2_
  247.3 40.1 %collective-permute-done.148.refs_1_ = bf16[720,2560]{1,0:T(8,128)(2,1)} collective-permute-done((bf16[720,2560]{1,0:T(8,128)(2,1)}, bf16[720,2560]{1,0:T(8,128)(2,1)}, u32[]{:S(2)}, u32[]{:S(2)}) %collective-permute-start.148) | collective-permute-done | bytes 3686432 | tf_op jit(solution)/shard_map/cond/branch_1_fun/ppermute | solution.py:264
  287.4 6.7 %mean_rows.16.refs_2_ = bf16[864,2560]{1,0:T(8,128)(2,1)} custom-call(bf16[720,2560]{1,0:T(8,128)(2,1)} %step_rows.13.refs_0_, bf16[720,2560]{1,0:T(8,128)(2,1)} %collective-permute-done.148.refs_1_, bf16[864,2560]{1,0:T(8,128)(2,1)S(1)} %mean_rows.15.refs_2_, bf16[864,2560]{1,0:T(8,128)(2,1)} %get-tuple-element.370.refs_3_), custom_call_target="tpu_custom_call" | custom-call | bytes 11059200 | tf_op jit(solution)/shard_map/cond/branch_1_fun/mean_rows/pallas_call | solution.py:170
  294.1 8.2 %collective-permute-done.147.refs_1_ = bf16[144,2560]{1,0:T(8,128)(2,1)} collective-permute-done((bf16[144,2560]{1,0:T(8,128)(2,1)}, bf16[144,2560]{1,0:T(8,128)(2,1)}, u32[]{:S(2)}, u32[]{:S(2)}) %collective-permute-start.147) | collective-permute-done | bytes 737312 | tf_op jit(solution)/shard_map/cond/branch_1_fun/ppermute | solution.py:264
  302.4 2.4 mean_rows.17
  (84 shorter events, 15.5 us)
Async XLA Ops:
  1.6 6.8 %copy-start.12 = (bf16[32,2560]{1,0:T(8,128)(2,1)S(1)}, bf16[32,2560]{1,0:T(8,128)(2,1)}, u32[]{:S(2)}) copy-start(bf16[32,2560]{1,0:T(8,128)(2,1)} %get-tuple-element.170.refs_0_.rest_1_) | copy-start | bytes 491524 | tf_op jit(solution)/shard_map/cond
  1.6 6.8 %copy-start.16 = (bf16[32,2560]{1,0:T(8,128)(2,1)S(1)}, bf16[32,2560]{1,0:T(8,128)(2,1)}, u32[]{:S(2)}) copy-start(bf16[32,2560]{1,0:T(8,128)(2,1)} %get-tuple-element.171.refs_8_) | copy-start | bytes 491524 | tf_op jit(solution)/shard_map/cond
  5.4 52.2 %collective-permute-start.144 = (bf16[432,2560]{1,0:T(8,128)(2,1)}, bf16[432,2560]{1,0:T(8,128)(2,1)}, u32[]{:S(2)}, u32[]{:S(2)}) collective-permute-start(bf16[432,2560]{1,0:T(8,128)(2,1)} %rows_of.4), channel_id=1, source_target_pairs={{0,16},{8,24},{16,0},{24,8},{1,17},{9,25},{17,1},{25,9},{2,18},{10... | collective-permute-start | bytes 6635528 | tf_op jit(solution)/shard_map/cond/branch_1_fun/ppermute | solution.py:264
  8.4 6.5 %collective-permute-start.42 = (bf16[32,2560]{1,0:T(8,128)(2,1)S(1)}, bf16[32,2560]{1,0:T(8,128)(2,1)}, u32[]{:S(2)}, u32[]{:S(2)}) collective-permute-start(bf16[32,2560]{1,0:T(8,128)(2,1)S(1)} %get-tuple-element.155), channel_id=1, source_target_pairs={{0,1},{2,0},{4,2},{6,4},{7,6},{5,7},{3,5},{1,3},{8,9},{10,8},{12,1... | collective-permute-start | bytes 491528 | tf_op jit(solution)/shard_map/cond/branch_1_fun/cond/branch_0_fun/ppermute | solution.py:267
  9.9 7.2 %collective-permute-start.52 = (bf16[32,2560]{1,0:T(8,128)(2,1)S(1)}, bf16[32,2560]{1,0:T(8,128)(2,1)}, u32[]{:S(2)}, u32[]{:S(2)}) collective-permute-start(bf16[32,2560]{1,0:T(8,128)(2,1)S(1)} %get-tuple-element.156), channel_id=1, source_target_pairs={{0,2},{2,4},{4,6},{6,7},{7,5},{5,3},{3,1},{1,0},{8,10},{10,12},{12... | collective-permute-start | bytes 491528 | tf_op jit(solution)/shard_map/cond/branch_1_fun/cond/branch_0_fun/ppermute | solution.py:267
  10.4 10.2 %collective-permute-start.46 = (bf16[32,2560]{1,0:T(8,128)(2,1)S(1)}, bf16[32,2560]{1,0:T(8,128)(2,1)}, u32[]{:S(2)}, u32[]{:S(2)}) collective-permute-start(bf16[32,2560]{1,0:T(8,128)(2,1)S(1)} %get-tuple-element.155), channel_id=1, source_target_pairs={{0,2},{2,4},{4,6},{6,7},{7,5},{5,3},{3,1},{1,0},{8,10},{10,12},{12... | collective-permute-start | bytes 491528 | tf_op jit(solution)/shard_map/cond/branch_1_fun/cond/branch_0_fun/ppermute | solution.py:267
  12.0 9.2 %collective-permute-start.49 = (bf16[32,2560]{1,0:T(8,128)(2,1)S(1)}, bf16[32,2560]{1,0:T(8,128)(2,1)}, u32[]{:S(2)}, u32[]{:S(2)}) collective-permute-start(bf16[32,2560]{1,0:T(8,128)(2,1)S(1)} %get-tuple-element.156), channel_id=1, source_target_pairs={{0,1},{2,0},{4,2},{6,4},{7,6},{5,7},{3,5},{1,3},{8,9},{10,8},{12,1... | collective-permute-start | bytes 491528 | tf_op jit(solution)/shard_map/cond/branch_1_fun/cond/branch_0_fun/ppermute | solution.py:267
  14.8 7.8 %collective-permute-start.43 = (bf16[32,2560]{1,0:T(8,128)(2,1)}, bf16[32,2560]{1,0:T(8,128)(2,1)}, u32[]{:S(2)}, u32[]{:S(2)}) collective-permute-start(bf16[32,2560]{1,0:T(8,128)(2,1)} %collective-permute-done.42), channel_id=1, source_target_pairs={{0,1},{2,0},{4,2},{6,4},{7,6},{5,7},{3,5},{1,3},{8,9},{10,8},{12,1... | collective-permute-start | bytes 491528 | tf_op jit(solution)/shard_map/cond/branch_1_fun/cond/branch_0_fun/ppermute | solution.py:267
  17.1 7.5 %collective-permute-start.53 = (bf16[32,2560]{1,0:T(8,128)(2,1)}, bf16[32,2560]{1,0:T(8,128)(2,1)}, u32[]{:S(2)}, u32[]{:S(2)}) collective-permute-start(bf16[32,2560]{1,0:T(8,128)(2,1)} %collective-permute-done.52), channel_id=1, source_target_pairs={{0,2},{2,4},{4,6},{6,7},{7,5},{5,3},{3,1},{1,0},{8,10},{10,12},{12... | collective-permute-start | bytes 491528 | tf_op jit(solution)/shard_map/cond/branch_1_fun/cond/branch_0_fun/ppermute | solution.py:267
  20.6 7.5 %collective-permute-start.47 = (bf16[32,2560]{1,0:T(8,128)(2,1)}, bf16[32,2560]{1,0:T(8,128)(2,1)}, u32[]{:S(2)}, u32[]{:S(2)}) collective-permute-start(bf16[32,2560]{1,0:T(8,128)(2,1)} %collective-permute-done.46), channel_id=1, source_target_pairs={{0,2},{2,4},{4,6},{6,7},{7,5},{5,3},{3,1},{1,0},{8,10},{10,12},{12... | collective-permute-start | bytes 491528 | tf_op jit(solution)/shard_map/cond/branch_1_fun/cond/branch_0_fun/ppermute | solution.py:267
  21.1 7.3 %collective-permute-start.50 = (bf16[32,2560]{1,0:T(8,128)(2,1)}, bf16[32,2560]{1,0:T(8,128)(2,1)}, u32[]{:S(2)}, u32[]{:S(2)}) collective-permute-start(bf16[32,2560]{1,0:T(8,128)(2,1)} %collective-permute-done.49), channel_id=1, source_target_pairs={{0,1},{2,0},{4,2},{6,4},{7,6},{5,7},{3,5},{1,3},{8,9},{10,8},{12,1... | collective-permute-start | bytes 491528 | tf_op jit(solution)/shard_map/cond/branch_1_fun/cond/branch_0_fun/ppermute | solution.py:267
  22.7 7.5 %collective-permute-start.44 = (bf16[32,2560]{1,0:T(8,128)(2,1)}, bf16[32,2560]{1,0:T(8,128)(2,1)}, u32[]{:S(2)}, u32[]{:S(2)}) collective-permute-start(bf16[32,2560]{1,0:T(8,128)(2,1)} %collective-permute-done.43), channel_id=1, source_target_pairs={{0,1},{2,0},{4,2},{6,4},{7,6},{5,7},{3,5},{1,3},{8,9},{10,8},{12,1... | collective-permute-start | bytes 491528 | tf_op jit(solution)/shard_map/cond/branch_1_fun/cond/branch_0_fun/ppermute | solution.py:267
  24.6 7.5 %collective-permute-start.54 = (bf16[32,2560]{1,0:T(8,128)(2,1)}, bf16[32,2560]{1,0:T(8,128)(2,1)}, u32[]{:S(2)}, u32[]{:S(2)}) collective-permute-start(bf16[32,2560]{1,0:T(8,128)(2,1)} %collective-permute-done.53), channel_id=1, source_target_pairs={{0,2},{2,4},{4,6},{6,7},{7,5},{5,3},{3,1},{1,0},{8,10},{10,12},{12... | collective-permute-start | bytes 491528 | tf_op jit(solution)/shard_map/cond/branch_1_fun/cond/branch_0_fun/ppermute | solution.py:267
  28.1 6.6 %collective-permute-start.48 = (bf16[32,2560]{1,0:T(8,128)(2,1)}, bf16[32,2560]{1,0:T(8,128)(2,1)}, u32[]{:S(2)}, u32[]{:S(2)}) collective-permute-start(bf16[32,2560]{1,0:T(8,128)(2,1)} %collective-permute-done.47), channel_id=1, source_target_pairs={{0,2},{2,4},{4,6},{6,7},{7,5},{5,3},{3,1},{1,0},{8,10},{10,12},{12... | collective-permute-start | bytes 491528 | tf_op jit(solution)/shard_map/cond/branch_1_fun/cond/branch_0_fun/ppermute | solution.py:267
  28.5 6.2 %collective-permute-start.51 = (bf16[32,2560]{1,0:T(8,128)(2,1)}, bf16[32,2560]{1,0:T(8,128)(2,1)}, u32[]{:S(2)}, u32[]{:S(2)}) collective-permute-start(bf16[32,2560]{1,0:T(8,128)(2,1)} %collective-permute-done.50), channel_id=1, source_target_pairs={{0,1},{2,0},{4,2},{6,4},{7,6},{5,7},{3,5},{1,3},{8,9},{10,8},{12,1... | collective-permute-start | bytes 491528 | tf_op jit(solution)/shard_map/cond/branch_1_fun/cond/branch_0_fun/ppermute | solution.py:267
  30.1 5.8 %collective-permute-start.45 = (bf16[32,2560]{1,0:T(8,128)(2,1)}, bf16[32,2560]{1,0:T(8,128)(2,1)}, u32[]{:S(2)}, u32[]{:S(2)}) collective-permute-start(bf16[32,2560]{1,0:T(8,128)(2,1)} %collective-permute-done.44), channel_id=1, source_target_pairs={{0,1},{2,0},{4,2},{6,4},{7,6},{5,7},{3,5},{1,3},{8,9},{10,8},{12,1... | collective-permute-start | bytes 491528 | tf_op jit(solution)/shard_map/cond/branch_1_fun/cond/branch_0_fun/ppermute | solution.py:267
  32.0 5.6 %collective-permute-start.55 = (bf16[32,2560]{1,0:T(8,128)(2,1)}, bf16[32,2560]{1,0:T(8,128)(2,1)}, u32[]{:S(2)}, u32[]{:S(2)}) collective-permute-start(bf16[32,2560]{1,0:T(8,128)(2,1)} %collective-permute-done.54), channel_id=1, source_target_pairs={{0,2},{2,4},{4,6},{6,7},{7,5},{5,3},{3,1},{1,0},{8,10},{10,12},{12... | collective-permute-start | bytes 491528 | tf_op jit(solution)/shard_map/cond/branch_1_fun/cond/branch_0_fun/ppermute | solution.py:267
  37.7 9.3 %slice-start.2 = ((s8[4423680]{0:T(1024)(128)(4,1)}), s8[4194304]{0:T(1024)(128)(4,1)S(1)}, s32[]{:S(2)}) async-start(s8[4423680]{0:T(1024)(128)(4,1)} %bitcast.27), calls=%async_computation.2 | async-start | bytes 8388608 | tf_op jit(solution)/shard_map/cond
  37.7 9.3 %slice-start.3 = ((s8[4423680]{0:T(1024)(128)(4,1)}), s8[229376]{0:T(1024)(128)(4,1)S(1)}, s32[]{:S(2)}) async-start(s8[4423680]{0:T(1024)(128)(4,1)} %bitcast.27), calls=%async_computation.3 | async-start | bytes 458752 | tf_op jit(solution)/shard_map/cond
  46.9 2.8 copy-start
  47.0 10.6 %copy-start.6 = (bf16[864,2560]{1,0:T(8,128)(2,1)S(1)}, bf16[864,2560]{1,0:T(8,128)(2,1)}, u32[]{:S(2)}) copy-start(bf16[864,2560]{1,0:T(8,128)(2,1)} %get-tuple-element.188.refs_18_.weight_ref.down_ref) | copy-start | bytes 13271044 | tf_op jit(solution)/shard_map/cond
  47.0 14.8 %slice-start.4 = ((s8[4423680]{0:T(1024)(128)(4,1)}), s8[4194304]{0:T(1024)(128)(4,1)S(1)}, s32[]{:S(2)}) async-start(s8[4423680]{0:T(1024)(128)(4,1)} %bitcast.31), calls=%async_computation.4 | async-start | bytes 8388608 | tf_op jit(solution)/shard_map/cond
  49.7 63.8 %collective-permute-start.145 = (bf16[464,2816]{1,0:T(8,128)(2,1)}, bf16[464,2816]{1,0:T(8,128)(2,1)S(1)}, u32[]{:S(2)}, u32[]{:S(2)}) collective-permute-start(bf16[464,2816]{1,0:T(8,128)(2,1)} %step_rows.11.refs_0_), channel_id=1, source_target_pairs={{0,16},{8,24},{16,0},{24,8},{1,17},{9,25},{17,1},{25,9},{2,18},{10... | collective-permute-start | bytes 7839752 | tf_op jit(solution)/shard_map/cond/branch_1_fun/ppermute | solution.py:264
  57.6 4.2 %slice-start.5 = ((s8[4423680]{0:T(1024)(128)(4,1)}), s8[229376]{0:T(1024)(128)(4,1)S(1)}, s32[]{:S(2)}) async-start(s8[4423680]{0:T(1024)(128)(4,1)} %bitcast.31), calls=%async_computation.5 | async-start | bytes 458752 | tf_op jit(solution)/shard_map/cond
  70.0 7.1 %copy-start.9 = (f32[256,2560]{1,0:T(8,128)S(1)}, f32[256,2560]{1,0:T(8,128)}, u32[]{:S(2)}) copy-start(f32[256,2560]{1,0:T(8,128)} %get-tuple-element.160) | copy-start | bytes 7864324
  70.1 7.0 %collective-permute-start.123 = (bf16[32,2560]{1,0:T(8,128)(2,1)S(1)}, bf16[32,2560]{1,0:T(8,128)(2,1)S(1)}, u32[]{:S(2)}, u32[]{:S(2)}) collective-permute-start(bf16[32,2560]{1,0:T(8,128)(2,1)S(1)} %get-tuple-element.253), channel_id=1, source_target_pairs={{0,1},{2,0},{4,2},{6,4},{7,6},{5,7},{3,5},{1,3},{8,9},{10,8},{12,1... | collective-permute-start | bytes 491528 | tf_op jit(solution)/shard_map/cond/branch_1_fun/cond/branch_0_fun/ppermute | solution.py:267
  72.2 9.9 %collective-permute-start.126 = (bf16[32,2560]{1,0:T(8,128)(2,1)S(1)}, bf16[32,2560]{1,0:T(8,128)(2,1)S(1)}, u32[]{:S(2)}, u32[]{:S(2)}) collective-permute-start(bf16[32,2560]{1,0:T(8,128)(2,1)S(1)} %get-tuple-element.254), channel_id=1, source_target_pairs={{0,2},{2,4},{4,6},{6,7},{7,5},{5,3},{3,1},{1,0},{8,10},{10,12},{12... | collective-permute-start | bytes 491528 | tf_op jit(solution)/shard_map/cond/branch_1_fun/cond/branch_0_fun/ppermute | solution.py:267
  72.5 8.1 %collective-permute-start.116 = (bf16[32,2560]{1,0:T(8,128)(2,1)S(1)}, bf16[32,2560]{1,0:T(8,128)(2,1)S(1)}, u32[]{:S(2)}, u32[]{:S(2)}) collective-permute-start(bf16[32,2560]{1,0:T(8,128)(2,1)S(1)} %get-tuple-element.255), channel_id=1, source_target_pairs={{0,1},{2,0},{4,2},{6,4},{7,6},{5,7},{3,5},{1,3},{8,9},{10,8},{12,1... | collective-permute-start | bytes 491528 | tf_op jit(solution)/shard_map/cond/branch_1_fun/cond/branch_0_fun/ppermute | solution.py:267
  74.5 17.3 %collective-permute-start.120 = (bf16[32,2560]{1,0:T(8,128)(2,1)S(1)}, bf16[32,2560]{1,0:T(8,128)(2,1)S(1)}, u32[]{:S(2)}, u32[]{:S(2)}) collective-permute-start(bf16[32,2560]{1,0:T(8,128)(2,1)S(1)} %get-tuple-element.256), channel_id=1, source_target_pairs={{0,2},{2,4},{4,6},{6,7},{7,5},{5,3},{3,1},{1,0},{8,10},{10,12},{12... | collective-permute-start | bytes 491528 | tf_op jit(solution)/shard_map/cond/branch_1_fun/cond/branch_0_fun/ppermute | solution.py:267
  77.1 6.4 %collective-permute-start.124 = (bf16[32,2560]{1,0:T(8,128)(2,1)S(1)}, bf16[32,2560]{1,0:T(8,128)(2,1)S(1)}, u32[]{:S(2)}, u32[]{:S(2)}) collective-permute-start(bf16[32,2560]{1,0:T(8,128)(2,1)S(1)} %add_convert_fusion.29), channel_id=1, source_target_pairs={{0,1},{2,0},{4,2},{6,4},{7,6},{5,7},{3,5},{1,3},{8,9},{10,8},{12,1... | collective-permute-start | bytes 491528 | tf_op jit(solution)/shard_map/cond/branch_1_fun/cond/branch_0_fun/ppermute | solution.py:267
  80.6 7.1 %collective-permute-start.117 = (bf16[32,2560]{1,0:T(8,128)(2,1)S(1)}, bf16[32,2560]{1,0:T(8,128)(2,1)S(1)}, u32[]{:S(2)}, u32[]{:S(2)}) collective-permute-start(bf16[32,2560]{1,0:T(8,128)(2,1)S(1)} %add_convert_fusion.35), channel_id=1, source_target_pairs={{0,1},{2,0},{4,2},{6,4},{7,6},{5,7},{3,5},{1,3},{8,9},{10,8},{12,1... | collective-permute-start | bytes 491528 | tf_op jit(solution)/shard_map/cond/branch_1_fun/cond/branch_0_fun/ppermute | solution.py:267
  83.6 6.6 %collective-permute-start.127 = (bf16[32,2560]{1,0:T(8,128)(2,1)S(1)}, bf16[32,2560]{1,0:T(8,128)(2,1)S(1)}, u32[]{:S(2)}, u32[]{:S(2)}) collective-permute-start(bf16[32,2560]{1,0:T(8,128)(2,1)S(1)} %get-tuple-element.250), channel_id=1, source_target_pairs={{0,2},{2,4},{4,6},{6,7},{7,5},{5,3},{3,1},{1,0},{8,10},{10,12},{12... | collective-permute-start | bytes 491528 | tf_op jit(solution)/shard_map/cond/branch_1_fun/cond/branch_0_fun/ppermute | solution.py:267
  85.1 16.8 %collective-permute-start.125 = (bf16[32,2560]{1,0:T(8,128)(2,1)S(1)}, bf16[32,2560]{1,0:T(8,128)(2,1)S(1)}, u32[]{:S(2)}, u32[]{:S(2)}) collective-permute-start(bf16[32,2560]{1,0:T(8,128)(2,1)S(1)} %get-tuple-element.249), channel_id=1, source_target_pairs={{0,1},{2,0},{4,2},{6,4},{7,6},{5,7},{3,5},{1,3},{8,9},{10,8},{12,1... | collective-permute-start | bytes 491528 | tf_op jit(solution)/shard_map/cond/branch_1_fun/cond/branch_0_fun/ppermute | solution.py:267
  87.8 5.7 %collective-permute-start.118 = (bf16[32,2560]{1,0:T(8,128)(2,1)S(1)}, bf16[32,2560]{1,0:T(8,128)(2,1)S(1)}, u32[]{:S(2)}, u32[]{:S(2)}) collective-permute-start(bf16[32,2560]{1,0:T(8,128)(2,1)S(1)} %add_convert_fusion.34), channel_id=1, source_target_pairs={{0,1},{2,0},{4,2},{6,4},{7,6},{5,7},{3,5},{1,3},{8,9},{10,8},{12,1... | collective-permute-start | bytes 491528 | tf_op jit(solution)/shard_map/cond/branch_1_fun/cond/branch_0_fun/ppermute | solution.py:267
  90.2 7.2 %collective-permute-start.128 = (bf16[32,2560]{1,0:T(8,128)(2,1)S(1)}, bf16[32,2560]{1,0:T(8,128)(2,1)S(1)}, u32[]{:S(2)}, u32[]{:S(2)}) collective-permute-start(bf16[32,2560]{1,0:T(8,128)(2,1)S(1)} %add_convert_fusion.26), channel_id=1, source_target_pairs={{0,2},{2,4},{4,6},{6,7},{7,5},{5,3},{3,1},{1,0},{8,10},{10,12},{12... | collective-permute-start | bytes 491528 | tf_op jit(solution)/shard_map/cond/branch_1_fun/cond/branch_0_fun/ppermute | solution.py:267
  93.5 7.1 %collective-permute-start.121 = (bf16[32,2560]{1,0:T(8,128)(2,1)S(1)}, bf16[32,2560]{1,0:T(8,128)(2,1)S(1)}, u32[]{:S(2)}, u32[]{:S(2)}) collective-permute-start(bf16[32,2560]{1,0:T(8,128)(2,1)S(1)} %get-tuple-element.252), channel_id=1, source_target_pairs={{0,2},{2,4},{4,6},{6,7},{7,5},{5,3},{3,1},{1,0},{8,10},{10,12},{12... | collective-permute-start | bytes 491528 | tf_op jit(solution)/shard_map/cond/branch_1_fun/cond/branch_0_fun/ppermute | solution.py:267
  95.0 8.5 %collective-permute-start.119 = (bf16[32,2560]{1,0:T(8,128)(2,1)S(1)}, bf16[32,2560]{1,0:T(8,128)(2,1)S(1)}, u32[]{:S(2)}, u32[]{:S(2)}) collective-permute-start(bf16[32,2560]{1,0:T(8,128)(2,1)S(1)} %get-tuple-element.251), channel_id=1, source_target_pairs={{0,1},{2,0},{4,2},{6,4},{7,6},{5,7},{3,5},{1,3},{8,9},{10,8},{12,1... | collective-permute-start | bytes 491528 | tf_op jit(solution)/shard_map/cond/branch_1_fun/cond/branch_0_fun/ppermute | solution.py:267
  97.4 5.4 %collective-permute-start.129 = (bf16[32,2560]{1,0:T(8,128)(2,1)S(1)}, bf16[32,2560]{1,0:T(8,128)(2,1)S(1)}, u32[]{:S(2)}, u32[]{:S(2)}) collective-permute-start(bf16[32,2560]{1,0:T(8,128)(2,1)S(1)} %add_convert_fusion.25), channel_id=1, source_target_pairs={{0,2},{2,4},{4,6},{6,7},{7,5},{5,3},{3,1},{1,0},{8,10},{10,12},{12... | collective-permute-start | bytes 491528 | tf_op jit(solution)/shard_map/cond/branch_1_fun/cond/branch_0_fun/ppermute | solution.py:267
  100.7 5.4 %collective-permute-start.122 = (bf16[32,2560]{1,0:T(8,128)(2,1)S(1)}, bf16[32,2560]{1,0:T(8,128)(2,1)S(1)}, u32[]{:S(2)}, u32[]{:S(2)}) collective-permute-start(bf16[32,2560]{1,0:T(8,128)(2,1)S(1)} %add_convert_fusion.31), channel_id=1, source_target_pairs={{0,2},{2,4},{4,6},{6,7},{7,5},{5,3},{3,1},{1,0},{8,10},{10,12},{12... | collective-permute-start | bytes 491528 | tf_op jit(solution)/shard_map/cond/branch_1_fun/cond/branch_0_fun/ppermute | solution.py:267
  106.4 7.1 %copy-start.13 = (bf16[32,2560]{1,0:T(8,128)(2,1)}, bf16[32,2560]{1,0:T(8,128)(2,1)S(1)}, u32[]{:S(2)}) copy-start(bf16[32,2560]{1,0:T(8,128)(2,1)S(1)} %get-tuple-element.366.rest_1_) | copy-start | bytes 491524 | tf_op jit(solution)/shard_map/cond
  106.4 101.9 %collective-permute-start.146 = (bf16[864,2560]{1,0:T(8,128)(2,1)}, bf16[864,2560]{1,0:T(8,128)(2,1)S(1)}, u32[]{:S(2)}, u32[]{:S(2)}) collective-permute-start(bf16[864,2560]{1,0:T(8,128)(2,1)} %step_rows.10.rest_0_), channel_id=1, source_target_pairs={{0,16},{8,24},{16,0},{24,8},{1,17},{9,25},{17,1},{25,9},{2,18},{10... | collective-permute-start | bytes 13271048 | tf_op jit(solution)/shard_map/cond/branch_1_fun/ppermute | solution.py:264
  113.5 1.3 copy-start.1
  114.8 98.0 %slice-start.8 = ((s8[4423680]{0:T(1024)(128)(4,1)}), s8[229376]{0:T(1024)(128)(4,1)S(1)}, s32[]{:S(2)}) async-start(s8[4423680]{0:T(1024)(128)(4,1)} %bitcast.38), calls=%async_computation.8 | async-start | bytes 458752 | tf_op jit(solution)/shard_map/cond
  121.1 91.7 %slice-start.9 = ((s8[4423680]{0:T(1024)(128)(4,1)}), s8[4194304]{0:T(1024)(128)(4,1)S(1)}, s32[]{:S(2)}) async-start(s8[4423680]{0:T(1024)(128)(4,1)} %bitcast.38), calls=%async_computation.9 | async-start | bytes 8388608 | tf_op jit(solution)/shard_map/cond
  121.1 166.3 %collective-permute-start.148 = (bf16[720,2560]{1,0:T(8,128)(2,1)}, bf16[720,2560]{1,0:T(8,128)(2,1)}, u32[]{:S(2)}, u32[]{:S(2)}) collective-permute-start(bf16[720,2560]{1,0:T(8,128)(2,1)} %step_rows.13.refs_0_), channel_id=1, source_target_pairs={{0,16},{8,24},{16,0},{24,8},{1,17},{9,25},{17,1},{25,9},{2,18},{10... | collective-permute-start | bytes 11059208 | tf_op jit(solution)/shard_map/cond/branch_1_fun/ppermute | solution.py:264
  210.7 91.7 %collective-permute-start.147 = (bf16[144,2560]{1,0:T(8,128)(2,1)}, bf16[144,2560]{1,0:T(8,128)(2,1)}, u32[]{:S(2)}, u32[]{:S(2)}) collective-permute-start(bf16[144,2560]{1,0:T(8,128)(2,1)} %step_rows.12.refs_13_.refs_0_), channel_id=1, source_target_pairs={{0,16},{8,24},{16,0},{24,8},{1,17},{9,25},{17,1},{25,9},{2,18},{10... | collective-permute-start | bytes 2211848 | tf_op jit(solution)/shard_map/cond/branch_1_fun/ppermute | solution.py:264
  212.8 5.8 %collective-permute-start.70 = (bf16[32,2560]{1,0:T(8,128)(2,1)S(1)}, bf16[32,2560]{1,0:T(8,128)(2,1)}, u32[]{:S(2)}, u32[]{:S(2)}) collective-permute-start(bf16[32,2560]{1,0:T(8,128)(2,1)S(1)} %get-tuple-element.163), channel_id=1, source_target_pairs={{0,1},{2,0},{4,2},{6,4},{7,6},{5,7},{3,5},{1,3},{8,9},{10,8},{12,1... | collective-permute-start | bytes 491528 | tf_op jit(solution)/shard_map/cond/branch_1_fun/cond/branch_0_fun/ppermute | solution.py:267
  214.4 6.1 %collective-permute-start.74 = (bf16[32,2560]{1,0:T(8,128)(2,1)S(1)}, bf16[32,2560]{1,0:T(8,128)(2,1)}, u32[]{:S(2)}, u32[]{:S(2)}) collective-permute-start(bf16[32,2560]{1,0:T(8,128)(2,1)S(1)} %get-tuple-element.163), channel_id=1, source_target_pairs={{0,2},{2,4},{4,6},{6,7},{7,5},{5,3},{3,1},{1,0},{8,10},{10,12},{12... | collective-permute-start | bytes 491528 | tf_op jit(solution)/shard_map/cond/branch_1_fun/cond/branch_0_fun/ppermute | solution.py:267
  218.7 6.9 %collective-permute-start.71 = (bf16[32,2560]{1,0:T(8,128)(2,1)}, bf16[32,2560]{1,0:T(8,128)(2,1)}, u32[]{:S(2)}, u32[]{:S(2)}) collective-permute-start(bf16[32,2560]{1,0:T(8,128)(2,1)} %collective-permute-done.70), channel_id=1, source_target_pairs={{0,1},{2,0},{4,2},{6,4},{7,6},{5,7},{3,5},{1,3},{8,9},{10,8},{12,1... | collective-permute-start | bytes 491528 | tf_op jit(solution)/shard_map/cond/branch_1_fun/cond/branch_0_fun/ppermute | solution.py:267
  220.5 7.2 %collective-permute-start.75 = (bf16[32,2560]{1,0:T(8,128)(2,1)}, bf16[32,2560]{1,0:T(8,128)(2,1)}, u32[]{:S(2)}, u32[]{:S(2)}) collective-permute-start(bf16[32,2560]{1,0:T(8,128)(2,1)} %collective-permute-done.74), channel_id=1, source_target_pairs={{0,2},{2,4},{4,6},{6,7},{7,5},{5,3},{3,1},{1,0},{8,10},{10,12},{12... | collective-permute-start | bytes 491528 | tf_op jit(solution)/shard_map/cond/branch_1_fun/cond/branch_0_fun/ppermute | solution.py:267
  225.6 7.0 %collective-permute-start.72 = (bf16[32,2560]{1,0:T(8,128)(2,1)}, bf16[32,2560]{1,0:T(8,128)(2,1)}, u32[]{:S(2)}, u32[]{:S(2)}) collective-permute-start(bf16[32,2560]{1,0:T(8,128)(2,1)} %collective-permute-done.71), channel_id=1, source_target_pairs={{0,1},{2,0},{4,2},{6,4},{7,6},{5,7},{3,5},{1,3},{8,9},{10,8},{12,1... | collective-permute-start | bytes 491528 | tf_op jit(solution)/shard_map/cond/branch_1_fun/cond/branch_0_fun/ppermute | solution.py:267
  227.7 9.9 %collective-permute-start.76 = (bf16[32,2560]{1,0:T(8,128)(2,1)}, bf16[32,2560]{1,0:T(8,128)(2,1)}, u32[]{:S(2)}, u32[]{:S(2)}) collective-permute-start(bf16[32,2560]{1,0:T(8,128)(2,1)} %collective-permute-done.75), channel_id=1, source_target_pairs={{0,2},{2,4},{4,6},{6,7},{7,5},{5,3},{3,1},{1,0},{8,10},{10,12},{12... | collective-permute-start | bytes 491528 | tf_op jit(solution)/shard_map/cond/branch_1_fun/cond/branch_0_fun/ppermute | solution.py:267
  232.6 5.6 %collective-permute-start.73 = (bf16[32,2560]{1,0:T(8,128)(2,1)}, bf16[32,2560]{1,0:T(8,128)(2,1)}, u32[]{:S(2)}, u32[]{:S(2)}) collective-permute-start(bf16[32,2560]{1,0:T(8,128)(2,1)} %collective-permute-done.72), channel_id=1, source_target_pairs={{0,1},{2,0},{4,2},{6,4},{7,6},{5,7},{3,5},{1,3},{8,9},{10,8},{12,1... | collective-permute-start | bytes 491528 | tf_op jit(solution)/shard_map/cond/branch_1_fun/cond/branch_0_fun/ppermute | solution.py:267
  238.2 1.3 copy-start.2
  247.3 46.8 %copy-start.8 = (bf16[864,2560]{1,0:T(8,128)(2,1)}, bf16[864,2560]{1,0:T(8,128)(2,1)S(1)}, u32[]{:S(2)}) copy-start(bf16[864,2560]{1,0:T(8,128)(2,1)S(1)} %mean_rows.15.refs_2_) | copy-start | bytes 13271044 | tf_op jit(solution)/shard_map/cond
  294.1 10.7 %copy-start.14 = (bf16[32,2560]{1,0:T(8,128)(2,1)S(1)}, bf16[32,2560]{1,0:T(8,128)(2,1)}, u32[]{:S(2)}) copy-start(bf16[32,2560]{1,0:T(8,128)(2,1)} %copy-done.13) | copy-start | bytes 491524 | tf_op jit(solution)/shard_map/cond
  304.8 0.7 copy-start.15
where the time goes:
time: 306 us; the launch traced here: 305 us
  waiting for transfers between devices  192 us (63%)
  Pallas kernels  55.4 us (18%)
  starting transfers between devices  49.6 us (16%)
  local copies, waits for them, and re-layouts  3.42 us (1%)
  other arithmetic  3.07 us (1%)
    ppermute x5, waiting for transfers between devices, send(): lax.ppermute(x, 'rep', [(i, (i + distance) % replicas) for i in range(rep...  146 us
    ppermute x35, waiting for transfers between devices, along(): lax.ppermute(x, 'tp', [(ring[i], ring[(i + by) % devices]) for i in range...  45.6 us
    ppermute x35, starting transfers between devices, along(): lax.ppermute(x, 'tp', [(ring[i], ring[(i + by) % devices]) for i in range...  40.4 us
    pallas_call x5, Pallas kernels, into_rows(): pl.pallas_call(with_others, grid=(rows // BLOCK,), in_specs=in_specs + [A...  20.3 us
    pallas_call x4, Pallas kernels, step_rows(): pl.pallas_call(body, grid=(steps if below is None else steps + 1,), in_sp...  15.6 us
    pallas_call x1, Pallas kernels, forward(): pl.pallas_call(body, grid=(units // block,), in_specs=[whole_spec(piece)...  9.23 us
    ppermute x5, starting transfers between devices, send(): lax.ppermute(x, 'rep', [(i, (i + distance) % replicas) for i in range(rep...  9.16 us
    pallas_call x1, Pallas kernels, partial_sums(): pl.pallas_call(body, grid=(steps,), in_specs=[rows_spec(0, count, block)]...  6.35 us
  transfers between devices with their start and end apart: 40, of which 29 were waited for; matrix products, arithmetic and copies ran while one was open for 1% of the time, Pallas kernels for 16%

commit v1 on v0

--- a/solution.py
+++ b/solution.py
@@ -18,7 +18,10 @@
 hidden_scale = 1.0 / math.sqrt(FF)
 
 ANY = pl.BlockSpec(memory_space=pl.ANY)
-PARAMS = pltpu.CompilerParams(vmem_limit_bytes=40 * 1024 * 1024)
+
+
+def vmem(mebibytes):
+    return pltpu.CompilerParams(vmem_limit_bytes=mebibytes * 1024 * 1024)
 
 
 def ring_of(devices):
@@ -91,7 +94,7 @@
         out_specs=[whole_spec(whole)] * 2 + [rows_spec(0, count, block)] * 3,
         out_shape=[whole] * 2 + [out] * 3,
         scratch_shapes=[pltpu.VMEM((D, count), jnp.bfloat16)] * 2,
-        compiler_params=PARAMS,
+        compiler_params=vmem(32),
         cost_estimate=cost(3, units, 3),
         name="forward",
     )(*pieces, gate_w, up_w, down_w)
@@ -134,7 +137,7 @@
         in_specs=specs + [ANY] * len(after),
         out_specs=rows_spec(0, width),
         out_shape=jax.ShapeDtypeStruct((out_rows, width), jnp.bfloat16),
-        compiler_params=PARAMS,
+        compiler_params=vmem(16),
         cost_estimate=costs or cost(1, rows, 2),
         name="step_rows",
     )(*ins, *after)
@@ -152,9 +155,32 @@
         in_specs=[rows_spec(at, block=block)],
         out_specs=rows_spec(block=block),
         out_shape=jax.ShapeDtypeStruct((rows, D), x.dtype),
-        compiler_params=PARAMS,
+        compiler_params=vmem(8),
         cost_estimate=cost(0, rows, 2),
         name="rows_of",
+    )(x)
+
+
+def first_rows(x, rows):
+    def body(x_ref, out_ref, sems):
+        copies = [
+            pltpu.make_async_copy(x_ref.at[pl.ds(at, BLOCK)], out_ref.at[pl.ds(at, BLOCK)], sems.at[at // BLOCK])
+            for at in range(0, rows, BLOCK)
+        ]
+        for copy in copies:
+            copy.start()
+        for copy in copies:
+            copy.wait()
+
+    return pl.pallas_call(
+        body,
+        in_specs=[ANY],
+        out_specs=pl.BlockSpec(memory_space=pltpu.VMEM),
+        out_shape=jax.ShapeDtypeStruct((rows, D), x.dtype),
+        scratch_shapes=[pltpu.SemaphoreType.DMA((rows // BLOCK,))],
+        compiler_params=vmem(8),
+        cost_estimate=cost(0, rows, 2),
+        name="first_rows",
     )(x)
 
 
@@ -175,7 +201,7 @@
         out_shape=jax.ShapeDtypeStruct((units, D), jnp.bfloat16),
         input_output_aliases={} if base is None else {len(ins): 0},
         scratch_shapes=scratch,
-        compiler_params=PARAMS,
+        compiler_params=vmem(16),
         cost_estimate=costs,
         name=name,
     )(*ins, *others)
@@ -248,7 +274,7 @@
         in_specs=[rows_spec(0, count, block)] * 3 + [rows_spec(block=block)] * 3 + [ANY] * len(after),
         out_specs=[whole_spec(out)] * 2,
         out_shape=[out] * 2,
-        compiler_params=PARAMS,
+        compiler_params=vmem(36),
         cost_estimate=cost(3, units, 3),
         name="partial_sums",
     )(hidden, d_gate, d_up, gate_w, up_w, down_w, *after)
@@ -268,7 +294,7 @@
 
     blocks = units // BLOCK
     raw = (blocks if distance == 1 else blocks // 2) * BLOCK
-    theirs_raw = send(up_w if raw == units else rows_of(up_w, 0, raw, BLOCK))
+    theirs_raw = send(up_w if raw == units else first_rows(up_w, raw))
 
     half = devices // 2
 

time: 306 us -> 156 us (0.51)
  waiting for transfers between devices: 192 us -> 60.7 us
  Pallas kernels: 55.4 us -> 46.6 us
  starting transfers between devices: 49.6 us -> 45.3 us
    ppermute x5 -> x4, waiting for transfers between devices: 146 us -> 14.6 us  [send(): lax.ppermute(x, 'rep', [(i, (i + distance) % replicas) for i in range(rep...]
    ppermute x5 -> x4, starting transfers between devices: 9.16 us -> 0.62 us  [send(): lax.ppermute(x, 'rep', [(i, (i + distance) % replicas) for i in range(rep...]
    pallas_call x4 -> x3, Pallas kernels: 15.6 us -> 8.33 us  [step_rows(): pl.pallas_call(body, grid=(steps if below is None else steps + 1,), in_sp...]
    ppermute x35, starting transfers between devices: 40.4 us -> 44.6 us  [along(): lax.ppermute(x, 'tp', [(ring[i], ring[(i + by) % devices]) for i in range...]
    pallas_call x5 -> x4, Pallas kernels: 20.3 us -> 23.1 us  [into_rows(): pl.pallas_call(with_others, grid=(rows // BLOCK,), in_specs=in_specs + [A...]
  transfers between devices with their start and end apart: 40 -> 39, of which waited for: 29 -> 27; matrix products, arithmetic and copies ran while one was open for 1% -> 0% of each run, Pallas kernels for 16% -> 29%
where the time goes in v1:
time: 156 us
  waiting for transfers between devices  60.7 us (39%)
  Pallas kernels  46.6 us (30%)
  starting transfers between devices  45.3 us (29%)
    ppermute x35, waiting for transfers between devices, along(): lax.ppermute(x, 'tp', [(ring[i], ring[(i + by) % devices]) for i in range...  46.1 us
    ppermute x35, starting transfers between devices, along(): lax.ppermute(x, 'tp', [(ring[i], ring[(i + by) % devices]) for i in range...  44.6 us
    pallas_call x4, Pallas kernels, into_rows(): pl.pallas_call(with_others, grid=(rows // BLOCK,), in_specs=in_specs + [A...  23.1 us
    ppermute x4, waiting for transfers between devices, send(): lax.ppermute(x, 'rep', [(i, (i + distance) % replicas) for i in range(rep...  14.6 us
    pallas_call x1, Pallas kernels, forward(): pl.pallas_call(body, grid=(units // block,), in_specs=[whole_spec(piece)...  9.32 us
    pallas_call x3, Pallas kernels, step_rows(): pl.pallas_call(body, grid=(steps if below is None else steps + 1,), in_sp...  8.33 us
    pallas_call x1, Pallas kernels, partial_sums(): pl.pallas_call(body, grid=(steps,), in_specs=[rows_spec(0, count, block)]...  4.89 us
  transfers between devices with their start and end apart: 39, of which 27 were waited for; matrix products, arithmetic and copies ran while one was open for 0% of the time, Pallas kernels for 29%

profile of v1, /device:TPU:0, one launch (start us, length us, event | category | flops | bytes accessed | tf_op | source)
XLA Modules:
  0.0 155.8 jit_solution(4814017081028719882)
XLA Ops:
  1.3 153.9 %conditional.21 = (bf16[32,2560]{1,0:T(8,128)(2,1)S(1)}, bf16[32,2560]{1,0:T(8,128)(2,1)}, bf16[864,2560]{1,0:T(8,128)(2,1)}, bf16[864,2560]{1,0:T(8,128)(2,1)}, bf16[864,2560]{1,0:T(8,128)(2,1)}) conditional(s32[]{:T(128)} %clamp.3, (pred[]{:T(512)}, bf16[32,2560]{1,0:T(8,128)(2,1)}, bf16[32,2560]{1,0:T(8,128)(2,1)}, bf16[864,2560]{1,0:T(8,128)(2,1)}, ...), branch_computations={%region_0.7_spmd, %region_7.14_spmd} | conditional | flops 33034731520 | bytes 468224352 | solution.py:396
  1.3 0.5 collective-permute-start.112
  1.8 31.1 %conditional.4 = (bf16[32,2560]{1,0:T(8,128)(2,1)}, bf16[32,2560]{1,0:T(8,128)(2,1)}, bf16[32,2560]{1,0:T(8,128)(2,1)}, bf16[32,2560]{1,0:T(8,128)(2,1)}, bf16[3...) conditional(s32[]{:T(128)} %convert_element_type.308, ...), branch_computations={%region_1.1_spmd, %region_2.2_spmd} | conditional | bytes 9175712 | solution.py:314
  1.8 2.7 %collective-permute-start.17 = (bf16[32,2560]{1,0:T(8,128)(2,1)}, bf16[32,2560]{1,0:T(8,128)(2,1)}, u32[]{:S(2)}, u32[]{:S(2)}) collective-permute-start(bf16[32,2560]{1,0:T(8,128)(2,1)} %get-tuple-element.106), channel_id=1, source_target_pairs={{0,2},{2,4},{4,6},{6,7},{7,5},{5,3},{3,1},{1,0},{8,10},{10,12},{12... | collective-permute-start | bytes 491528 | tf_op jit(solution)/shard_map/cond/branch_0_fun/cond/branch_1_fun/ppermute | solution.py:293
  4.5 2.0 %collective-permute-start.14 = (bf16[32,2560]{1,0:T(8,128)(2,1)}, bf16[32,2560]{1,0:T(8,128)(2,1)}, u32[]{:S(2)}, u32[]{:S(2)}) collective-permute-start(bf16[32,2560]{1,0:T(8,128)(2,1)} %get-tuple-element.106), channel_id=1, source_target_pairs={{0,1},{2,0},{4,2},{6,4},{7,6},{5,7},{3,5},{1,3},{8,9},{10,8},{12,1... | collective-permute-start | bytes 491528 | tf_op jit(solution)/shard_map/cond/branch_0_fun/cond/branch_1_fun/ppermute | solution.py:293
  6.6 2.4 %collective-permute-done.17 = bf16[32,2560]{1,0:T(8,128)(2,1)} collective-permute-done((bf16[32,2560]{1,0:T(8,128)(2,1)}, bf16[32,2560]{1,0:T(8,128)(2,1)}, u32[]{:S(2)}, u32[]{:S(2)}) %collective-permute-start.17) | collective-permute-done | bytes 163872 | tf_op jit(solution)/shard_map/cond/branch_0_fun/cond/branch_1_fun/ppermute | solution.py:293
  8.9 2.5 %collective-permute-start.18 = (bf16[32,2560]{1,0:T(8,128)(2,1)}, bf16[32,2560]{1,0:T(8,128)(2,1)}, u32[]{:S(2)}, u32[]{:S(2)}) collective-permute-start(bf16[32,2560]{1,0:T(8,128)(2,1)} %collective-permute-done.17), channel_id=1, source_target_pairs={{0,2},{2,4},{4,6},{6,7},{7,5},{5,3},{3,1},{1,0},{8,10},{10,12},{12... | collective-permute-start | bytes 491528 | tf_op jit(solution)/shard_map/cond/branch_0_fun/cond/branch_1_fun/ppermute | solution.py:293
  11.6 3.5 %collective-permute-done.14 = bf16[32,2560]{1,0:T(8,128)(2,1)} collective-permute-done((bf16[32,2560]{1,0:T(8,128)(2,1)}, bf16[32,2560]{1,0:T(8,128)(2,1)}, u32[]{:S(2)}, u32[]{:S(2)}) %collective-permute-start.14) | collective-permute-done | bytes 163872 | tf_op jit(solution)/shard_map/cond/branch_0_fun/cond/branch_1_fun/ppermute | solution.py:293
  15.1 2.1 %collective-permute-start.26 = (bf16[32,2560]{1,0:T(8,128)(2,1)}, bf16[32,2560]{1,0:T(8,128)(2,1)}, u32[]{:S(2)}, u32[]{:S(2)}) collective-permute-start(bf16[32,2560]{1,0:T(8,128)(2,1)} %collective-permute-done.25), channel_id=1, source_target_pairs={{0,2},{2,4},{4,6},{6,7},{7,5},{5,3},{3,1},{1,0},{8,10},{10,12},{12... | collective-permute-start | bytes 491528 | tf_op jit(solution)/shard_map/cond/branch_0_fun/cond/branch_1_fun/ppermute | solution.py:293
  17.2 1.7 %collective-permute-start.19 = (bf16[32,2560]{1,0:T(8,128)(2,1)}, bf16[32,2560]{1,0:T(8,128)(2,1)}, u32[]{:S(2)}, u32[]{:S(2)}) collective-permute-start(bf16[32,2560]{1,0:T(8,128)(2,1)} %collective-permute-done.18), channel_id=1, source_target_pairs={{0,2},{2,4},{4,6},{6,7},{7,5},{5,3},{3,1},{1,0},{8,10},{10,12},{12... | collective-permute-start | bytes 491528 | tf_op jit(solution)/shard_map/cond/branch_0_fun/cond/branch_1_fun/ppermute | solution.py:293
  19.2 3.4 %collective-permute-done.15 = bf16[32,2560]{1,0:T(8,128)(2,1)} collective-permute-done((bf16[32,2560]{1,0:T(8,128)(2,1)}, bf16[32,2560]{1,0:T(8,128)(2,1)}, u32[]{:S(2)}, u32[]{:S(2)}) %collective-permute-start.15) | collective-permute-done | bytes 163872 | tf_op jit(solution)/shard_map/cond/branch_0_fun/cond/branch_1_fun/ppermute | solution.py:293
  22.6 2.0 %collective-permute-start.27 = (bf16[32,2560]{1,0:T(8,128)(2,1)}, bf16[32,2560]{1,0:T(8,128)(2,1)}, u32[]{:S(2)}, u32[]{:S(2)}) collective-permute-start(bf16[32,2560]{1,0:T(8,128)(2,1)} %collective-permute-done.26), channel_id=1, source_target_pairs={{0,2},{2,4},{4,6},{6,7},{7,5},{5,3},{3,1},{1,0},{8,10},{10,12},{12... | collective-permute-start | bytes 491528 | tf_op jit(solution)/shard_map/cond/branch_0_fun/cond/branch_1_fun/ppermute | solution.py:293
  24.6 0.9 collective-permute-done.19
  25.6 1.7 %collective-permute-start.20 = (bf16[32,2560]{1,0:T(8,128)(2,1)}, bf16[32,2560]{1,0:T(8,128)(2,1)}, u32[]{:S(2)}, u32[]{:S(2)}) collective-permute-start(bf16[32,2560]{1,0:T(8,128)(2,1)} %collective-permute-done.19), channel_id=1, source_target_pairs={{0,2},{2,4},{4,6},{6,7},{7,5},{5,3},{3,1},{1,0},{8,10},{10,12},{12... | collective-permute-start | bytes 491528 | tf_op jit(solution)/shard_map/cond/branch_0_fun/cond/branch_1_fun/ppermute | solution.py:293
  27.3 0.3 collective-permute-start.24
  27.6 2.2 %collective-permute-done.16 = bf16[32,2560]{1,0:T(8,128)(2,1)} collective-permute-done((bf16[32,2560]{1,0:T(8,128)(2,1)}, bf16[32,2560]{1,0:T(8,128)(2,1)}, u32[]{:S(2)}, u32[]{:S(2)}) %collective-permute-start.16) | collective-permute-done | bytes 163872 | tf_op jit(solution)/shard_map/cond/branch_0_fun/cond/branch_1_fun/ppermute | solution.py:293
  29.7 0.3 collective-permute-done.27
  30.0 2.5 %collective-permute-done.20 = bf16[32,2560]{1,0:T(8,128)(2,1)} collective-permute-done((bf16[32,2560]{1,0:T(8,128)(2,1)}, bf16[32,2560]{1,0:T(8,128)(2,1)}, u32[]{:S(2)}, u32[]{:S(2)}) %collective-permute-start.20) | collective-permute-done | bytes 163872 | tf_op jit(solution)/shard_map/cond/branch_0_fun/cond/branch_1_fun/ppermute | solution.py:293
  32.5 0.5 collective-permute-done.24
  33.0 9.3 %forward.2 = (bf16[256,2560]{1,0:T(8,128)(2,1)S(1)}, bf16[256,2560]{1,0:T(8,128)(2,1)S(1)}, bf16[864,256]{1,0:T(8,128)(2,1)S(1)}, bf16[864,256]{1,0:T(8,128)(2,1)S(1)}, bf16[864,256]{1,0:T(8,128)(2,1)S(1)}) custom-call(bf16[32,2560]{1,0:T(8,128)(2,1)} %get-tuple-element.119.refs_0_.rest_1_, bf16[32,2560]{1,0:T(8,128)(2,1)} %get-tuple-element.121.refs_1_, ...), custom_call_target="tpu_custom_call" | custom-call | flops 3397386240 | bytes 13271040 | tf_op jit(solution)/shard_map/cond/branch_0_fun/forward/pallas_call | solution.py:90
  42.4 4.8 %step_rows.8 = bf16[896,2816]{1,0:T(8,128)(2,1)} custom-call(bf16[864,2560]{1,0:T(8,128)(2,1)S(1)} %bitcast.36, bf16[864,256]{1,0:T(8,128)(2,1)S(1)} %get-tuple-element.138.hidden_ref.left_ref, bf16[256,2560]{1,0:T(8,128)(2,1)S(1)} %get-tuple-element.144.right_ref, bf16[864,256]{1,0:T(8,128)(2,1)S(1)} %get-tuple-element.140.d_up_ref.rest_0_.refs_1_, ...), custom_call_target="tpu_custom_call" | custom-call | flops 1132462080 | bytes 8847360 | tf_op jit(solution)/shard_map/cond/branch_0_fun/step_rows/pallas_call | solution.py:134
  47.1 5.6 %collective-permute-done.112.rest_0_.refs_3_ = bf16[864,2560]{1,0:T(8,128)(2,1)} collective-permute-done((bf16[864,2560]{1,0:T(8,128)(2,1)}, bf16[864,2560]{1,0:T(8,128)(2,1)}, u32[]{:S(2)}, u32[]{:S(2)}) %collective-permute-start.112) | collective-permute-done | bytes 4423712 | tf_op jit(solution)/shard_map/cond/branch_0_fun/ppermute | solution.py:290
  52.7 2.1 %step_rows.7.rest_0_.refs_0_ = bf16[720,2560]{1,0:T(8,128)(2,1)S(1)} custom-call(bf16[864,2560]{1,0:T(8,128)(2,1)S(1)} %copy-done.5, bf16[864,256]{1,0:T(8,128)(2,1)S(1)} %get-tuple-element.139.left_ref.d_gate_ref, bf16[256,2560]{1,0:T(8,128)(2,1)S(1)} %get-tuple-element.141.right_ref.refs_2_, bf16[864,2560]{1,0:T(8,128)(2,1)} %collective-permute-done.112.rest_0_.refs_3_), custom_call_target="tpu_custom_call" | custom-call | flops 22649241600 | bytes 176947200 | tf_op jit(solution)/shard_map/cond/branch_0_fun/step_rows/pallas_call | solution.py:134
  54.8 4.9 %partial_sums.2 = (f32[256,2560]{1,0:T(8,128)S(1)}, f32[256,2560]{1,0:T(8,128)S(1)}) custom-call(bf16[864,256]{1,0:T(8,128)(2,1)S(1)} %get-tuple-element.138.hidden_ref.left_ref, bf16[864,256]{1,0:T(8,128)(2,1)S(1)} %get-tuple-element.139.left_ref.d_gate_ref, bf16[864,256]{1,0:T(8,128)(2,1)S(1)} %get-tuple-element.140.d_up_ref.rest_0_.refs_1_, ...), custom_call_target="tpu_custom_call" | custom-call | flops 3397386240 | bytes 13271040 | tf_op jit(solution)/shard_map/cond/branch_0_fun/partial_sums/pallas_call | solution.py:271
  59.7 38.3 %conditional.22 = (bf16[32,2560]{1,0:T(8,128)(2,1)S(1)}, bf16[32,2560]{1,0:T(8,128)(2,1)S(1)}) conditional(s32[]{:T(128)} %convert_element_type.308, (f32[256,2560]{1,0:T(8,128)S(1)}, f32[256,2560]{1,0:T(8,128)S(1)}) %partial_sums.2, (f32[256,2560]{1,0:T(8,128)S(1)}, f32[256,2560]{1,0:T(8,128)S(1)}) %partial_sums.2), branch_computations={%region_3.3_spmd, %region_4.4_spmd} | conditional | flops 4587520 | bytes 26542656
  59.9 2.4 %collective-permute-start.105 = (bf16[32,2560]{1,0:T(8,128)(2,1)S(1)}, bf16[32,2560]{1,0:T(8,128)(2,1)S(1)}, u32[]{:S(2)}, u32[]{:S(2)}) collective-permute-start(bf16[32,2560]{1,0:T(8,128)(2,1)S(1)} %get-tuple-element.245), channel_id=1, source_target_pairs={{0,2},{2,4},{4,6},{6,7},{7,5},{5,3},{3,1},{1,0},{8,10},{10,12},{12... | collective-permute-start | bytes 491528 | tf_op jit(solution)/shard_map/cond/branch_0_fun/cond/branch_1_fun/ppermute | solution.py:293
  62.6 2.1 %collective-permute-start.98 = (bf16[32,2560]{1,0:T(8,128)(2,1)S(1)}, bf16[32,2560]{1,0:T(8,128)(2,1)S(1)}, u32[]{:S(2)}, u32[]{:S(2)}) collective-permute-start(bf16[32,2560]{1,0:T(8,128)(2,1)S(1)} %get-tuple-element.247), channel_id=1, source_target_pairs={{0,2},{2,4},{4,6},{6,7},{7,5},{5,3},{3,1},{1,0},{8,10},{10,12},{12... | collective-permute-start | bytes 491528 | tf_op jit(solution)/shard_map/cond/branch_0_fun/cond/branch_1_fun/ppermute | solution.py:293
  64.6 2.8 %collective-permute-done.105 = bf16[32,2560]{1,0:T(8,128)(2,1)S(1)} collective-permute-done((bf16[32,2560]{1,0:T(8,128)(2,1)S(1)}, bf16[32,2560]{1,0:T(8,128)(2,1)S(1)}, u32[]{:S(2)}, u32[]{:S(2)}) %collective-permute-start.105) | collective-permute-done | bytes 163872 | tf_op jit(solution)/shard_map/cond/branch_0_fun/cond/branch_1_fun/ppermute | solution.py:293
  67.5 2.1 %collective-permute-start.106 = (bf16[32,2560]{1,0:T(8,128)(2,1)S(1)}, bf16[32,2560]{1,0:T(8,128)(2,1)S(1)}, u32[]{:S(2)}, u32[]{:S(2)}) collective-permute-start(bf16[32,2560]{1,0:T(8,128)(2,1)S(1)} %add_convert_fusion.17), channel_id=1, source_target_pairs={{0,2},{2,4},{4,6},{6,7},{7,5},{5,3},{3,1},{1,0},{8,10},{10,12},{12... | collective-permute-start | bytes 491528 | tf_op jit(solution)/shard_map/cond/branch_0_fun/cond/branch_1_fun/ppermute | solution.py:293
  69.6 1.3 collective-permute-done.98
  71.0 2.1 %collective-permute-start.99 = (bf16[32,2560]{1,0:T(8,128)(2,1)S(1)}, bf16[32,2560]{1,0:T(8,128)(2,1)S(1)}, u32[]{:S(2)}, u32[]{:S(2)}) collective-permute-start(bf16[32,2560]{1,0:T(8,128)(2,1)S(1)} %add_convert_fusion.23), channel_id=1, source_target_pairs={{0,2},{2,4},{4,6},{6,7},{7,5},{5,3},{3,1},{1,0},{8,10},{10,12},{12... | collective-permute-start | bytes 491528 | tf_op jit(solution)/shard_map/cond/branch_0_fun/cond/branch_1_fun/ppermute | solution.py:293
  73.1 1.6 collective-permute-done.106
  74.7 1.7 %collective-permute-start.109 = (bf16[32,2560]{1,0:T(8,128)(2,1)S(1)}, bf16[32,2560]{1,0:T(8,128)(2,1)S(1)}, u32[]{:S(2)}, u32[]{:S(2)}) collective-permute-start(bf16[32,2560]{1,0:T(8,128)(2,1)S(1)} %get-tuple-element.242), channel_id=1, source_target_pairs={{0,1},{2,0},{4,2},{6,4},{7,6},{5,7},{3,5},{1,3},{8,9},{10,8},{12,1... | collective-permute-start | bytes 491528 | tf_op jit(solution)/shard_map/cond/branch_0_fun/cond/branch_1_fun/ppermute | solution.py:293
  76.4 0.4 collective-permute-start.107
  76.8 0.9 collective-permute-done.99
  77.8 2.5 %collective-permute-start.100 = (bf16[32,2560]{1,0:T(8,128)(2,1)S(1)}, bf16[32,2560]{1,0:T(8,128)(2,1)S(1)}, u32[]{:S(2)}, u32[]{:S(2)}) collective-permute-start(bf16[32,2560]{1,0:T(8,128)(2,1)S(1)} %add_convert_fusion.22), channel_id=1, source_target_pairs={{0,2},{2,4},{4,6},{6,7},{7,5},{5,3},{3,1},{1,0},{8,10},{10,12},{12... | collective-permute-start | bytes 491528 | tf_op jit(solution)/shard_map/cond/branch_0_fun/cond/branch_1_fun/ppermute | solution.py:293
  80.3 1.0 collective-permute-done.109
  81.3 2.1 %collective-permute-start.110 = (bf16[32,2560]{1,0:T(8,128)(2,1)S(1)}, bf16[32,2560]{1,0:T(8,128)(2,1)S(1)}, u32[]{:S(2)}, u32[]{:S(2)}) collective-permute-start(bf16[32,2560]{1,0:T(8,128)(2,1)S(1)} %add_convert_fusion.14), channel_id=1, source_target_pairs={{0,1},{2,0},{4,2},{6,4},{7,6},{5,7},{3,5},{1,3},{8,9},{10,8},{12,1... | collective-permute-start | bytes 491528 | tf_op jit(solution)/shard_map/cond/branch_0_fun/cond/branch_1_fun/ppermute | solution.py:293
  83.6 1.9 %collective-permute-start.103 = (bf16[32,2560]{1,0:T(8,128)(2,1)S(1)}, bf16[32,2560]{1,0:T(8,128)(2,1)S(1)}, u32[]{:S(2)}, u32[]{:S(2)}) collective-permute-start(bf16[32,2560]{1,0:T(8,128)(2,1)S(1)} %get-tuple-element.244), channel_id=1, source_target_pairs={{0,1},{2,0},{4,2},{6,4},{7,6},{5,7},{3,5},{1,3},{8,9},{10,8},{12,1... | collective-permute-start | bytes 491528 | tf_op jit(solution)/shard_map/cond/branch_0_fun/cond/branch_1_fun/ppermute | solution.py:293
  85.5 0.3 collective-permute-start.101
  85.8 3.1 %collective-permute-done.110 = bf16[32,2560]{1,0:T(8,128)(2,1)S(1)} collective-permute-done((bf16[32,2560]{1,0:T(8,128)(2,1)S(1)}, bf16[32,2560]{1,0:T(8,128)(2,1)S(1)}, u32[]{:S(2)}, u32[]{:S(2)}) %collective-permute-start.110) | collective-permute-done | bytes 163872 | tf_op jit(solution)/shard_map/cond/branch_0_fun/cond/branch_1_fun/ppermute | solution.py:293
  88.9 1.7 %collective-permute-start.111 = (bf16[32,2560]{1,0:T(8,128)(2,1)S(1)}, bf16[32,2560]{1,0:T(8,128)(2,1)S(1)}, u32[]{:S(2)}, u32[]{:S(2)}) collective-permute-start(bf16[32,2560]{1,0:T(8,128)(2,1)S(1)} %add_convert_fusion.13), channel_id=1, source_target_pairs={{0,1},{2,0},{4,2},{6,4},{7,6},{5,7},{3,5},{1,3},{8,9},{10,8},{12,1... | collective-permute-start | bytes 491528 | tf_op jit(solution)/shard_map/cond/branch_0_fun/cond/branch_1_fun/ppermute | solution.py:293
  90.6 1.7 %collective-permute-done.103 = bf16[32,2560]{1,0:T(8,128)(2,1)S(1)} collective-permute-done((bf16[32,2560]{1,0:T(8,128)(2,1)S(1)}, bf16[32,2560]{1,0:T(8,128)(2,1)S(1)}, u32[]{:S(2)}, u32[]{:S(2)}) %collective-permute-start.103) | collective-permute-done | bytes 163872 | tf_op jit(solution)/shard_map/cond/branch_0_fun/cond/branch_1_fun/ppermute | solution.py:293
  92.4 1.5 collective-permute-start.104
  93.9 0.7 collective-permute-done.111
  94.7 3.1 %collective-permute-done.104 = bf16[32,2560]{1,0:T(8,128)(2,1)S(1)} collective-permute-done((bf16[32,2560]{1,0:T(8,128)(2,1)S(1)}, bf16[32,2560]{1,0:T(8,128)(2,1)S(1)}, u32[]{:S(2)}, u32[]{:S(2)}) %collective-permute-start.104) | collective-permute-done | bytes 163872 | tf_op jit(solution)/shard_map/cond/branch_0_fun/cond/branch_1_fun/ppermute | solution.py:293
  98.1 8.7 %collective-permute-done.113.x_ref.rest_0_.refs_4_ = bf16[896,2816]{1,0:T(8,128)(2,1)} collective-permute-done((bf16[896,2816]{1,0:T(8,128)(2,1)}, bf16[896,2816]{1,0:T(8,128)(2,1)}, u32[]{:S(2)}, u32[]{:S(2)}) %collective-permute-start.113) | collective-permute-done | bytes 5046304 | tf_op jit(solution)/shard_map/cond/branch_0_fun/ppermute | solution.py:290
  106.8 1.5 step_rows.9.refs_13_.refs_0_
  108.4 0.9 rows_of.2.refs_5_
  109.4 29.6 %conditional.11 = (bf16[32,2560]{1,0:T(8,128)(2,1)}, bf16[32,2560]{1,0:T(8,128)(2,1)}, bf16[32,2560]{1,0:T(8,128)(2,1)}, bf16[32,2560]{1,0:T(8,128)(2,1)}, bf16[...) conditional(s32[]{:T(128)} %convert_element_type.308, ...), branch_computations={%region_5.5_spmd, %region_6.6_spmd} | conditional | bytes 17858904 | solution.py:325
  109.4 2.4 %collective-permute-start.38 = (bf16[32,2560]{1,0:T(8,128)(2,1)S(1)}, bf16[32,2560]{1,0:T(8,128)(2,1)}, u32[]{:S(2)}, u32[]{:S(2)}) collective-permute-start(bf16[32,2560]{1,0:T(8,128)(2,1)S(1)} %get-tuple-element.115), channel_id=1, source_target_pairs={{0,2},{2,4},{4,6},{6,7},{7,5},{5,3},{3,1},{1,0},{8,10},{10,12},{12... | collective-permute-start | bytes 491528 | tf_op jit(solution)/shard_map/cond/branch_0_fun/cond/branch_1_fun/ppermute | solution.py:293
  111.8 4.0 %collective-permute-done.38 = bf16[32,2560]{1,0:T(8,128)(2,1)} collective-permute-done((bf16[32,2560]{1,0:T(8,128)(2,1)S(1)}, bf16[32,2560]{1,0:T(8,128)(2,1)}, u32[]{:S(2)}, u32[]{:S(2)}) %collective-permute-start.38) | collective-permute-done | bytes 163872 | tf_op jit(solution)/shard_map/cond/branch_0_fun/cond/branch_1_fun/ppermute | solution.py:293
  115.8 2.6 %collective-permute-start.39 = (bf16[32,2560]{1,0:T(8,128)(2,1)}, bf16[32,2560]{1,0:T(8,128)(2,1)}, u32[]{:S(2)}, u32[]{:S(2)}) collective-permute-start(bf16[32,2560]{1,0:T(8,128)(2,1)} %collective-permute-done.38), channel_id=1, source_target_pairs={{0,2},{2,4},{4,6},{6,7},{7,5},{5,3},{3,1},{1,0},{8,10},{10,12},{12... | collective-permute-start | bytes 491528 | tf_op jit(solution)/shard_map/cond/branch_0_fun/cond/branch_1_fun/ppermute | solution.py:293
  118.7 5.1 %collective-permute-done.39 = bf16[32,2560]{1,0:T(8,128)(2,1)} collective-permute-done((bf16[32,2560]{1,0:T(8,128)(2,1)}, bf16[32,2560]{1,0:T(8,128)(2,1)}, u32[]{:S(2)}, u32[]{:S(2)}) %collective-permute-start.39) | collective-permute-done | bytes 163872 | tf_op jit(solution)/shard_map/cond/branch_0_fun/cond/branch_1_fun/ppermute | solution.py:293
  123.7 1.8 %collective-permute-start.40 = (bf16[32,2560]{1,0:T(8,128)(2,1)}, bf16[32,2560]{1,0:T(8,128)(2,1)}, u32[]{:S(2)}, u32[]{:S(2)}) collective-permute-start(bf16[32,2560]{1,0:T(8,128)(2,1)} %collective-permute-done.39), channel_id=1, source_target_pairs={{0,2},{2,4},{4,6},{6,7},{7,5},{5,3},{3,1},{1,0},{8,10},{10,12},{12... | collective-permute-start | bytes 491528 | tf_op jit(solution)/shard_map/cond/branch_0_fun/cond/branch_1_fun/ppermute | solution.py:293
  125.5 0.3 collective-permute-start.37
  125.8 4.4 %collective-permute-done.40 = bf16[32,2560]{1,0:T(8,128)(2,1)} collective-permute-done((bf16[32,2560]{1,0:T(8,128)(2,1)}, bf16[32,2560]{1,0:T(8,128)(2,1)}, u32[]{:S(2)}, u32[]{:S(2)}) %collective-permute-start.40) | collective-permute-done | bytes 163872 | tf_op jit(solution)/shard_map/cond/branch_0_fun/cond/branch_1_fun/ppermute | solution.py:293
  130.2 1.5 collective-permute-start.41
  131.8 7.2 %mean_rows.10 = bf16[864,2560]{1,0:T(8,128)(2,1)} custom-call(bf16[896,2816]{1,0:T(8,128)(2,1)} %get-tuple-element.116.refs_0_, bf16[896,2816]{1,0:T(8,128)(2,1)} %get-tuple-element.117.refs_1_), custom_call_target="tpu_custom_call" | custom-call | bytes 13271040 | tf_op jit(solution)/shard_map/cond/branch_0_fun/cond/branch_1_fun/mean_rows/pallas_call | solution.py:196
  139.0 8.6 %mean_of_steps.2.refs_2_ = bf16[864,2560]{1,0:T(8,128)(2,1)S(1)} custom-call(bf16[864,2560]{1,0:T(8,128)(2,1)} %get-tuple-element.136.refs_17_.up_ref.refs_0_, bf16[864,256]{1,0:T(8,128)(2,1)S(1)} %get-tuple-element.140.d_up_ref.rest_0_.refs_1_, bf16[256,2560]{1,0:T(8,128)(2,1)S(1)} %get-tuple-element.141.right_ref.refs_2_, ...), custom_call_target="tpu_custom_call" | custom-call | flops 2264924160 | bytes 13271040 | tf_op jit(solution)/shard_map/cond/branch_0_fun/mean_of_steps/pallas_call | solution.py:196
  147.7 6.2 %mean_rows.11.refs_2_ = bf16[864,2560]{1,0:T(8,128)(2,1)} custom-call(bf16[720,2560]{1,0:T(8,128)(2,1)S(1)} %copy-done.4, bf16[720,2560]{1,0:T(8,128)(2,1)} %collective-permute-done.115.refs_1_, bf16[864,2560]{1,0:T(8,128)(2,1)S(1)} %mean_of_steps.2.refs_2_, bf16[864,2560]{1,0:T(8,128)(2,1)} %get-tuple-element.365.refs_3_), custom_call_target="tpu_custom_call" | custom-call | bytes 11059200 | tf_op jit(solution)/shard_map/cond/branch_0_fun/mean_rows/pallas_call | solution.py:196
  153.8 0.3 collective-permute-done.114.refs_1_
  154.1 1.1 mean_rows.12
  155.2 0.7 copy-done.14
  (66 shorter events, 2.1 us)
Async XLA Ops:
  1.3 51.4 %collective-permute-start.112 = (bf16[864,2560]{1,0:T(8,128)(2,1)}, bf16[864,2560]{1,0:T(8,128)(2,1)}, u32[]{:S(2)}, u32[]{:S(2)}) collective-permute-start(bf16[864,2560]{1,0:T(8,128)(2,1)} %get-tuple-element.136.refs_17_.up_ref.refs_0_), channel_id=1, source_target_pairs={{0,8},{8,16},{16,24},{24,0},{1,9},{9,17},{17,25},{25,1},{2,10},{10... | collective-permute-start | bytes 13271048 | tf_op jit(solution)/shard_map/cond/branch_0_fun/ppermute | solution.py:290
  1.8 7.1 %collective-permute-start.17 = (bf16[32,2560]{1,0:T(8,128)(2,1)}, bf16[32,2560]{1,0:T(8,128)(2,1)}, u32[]{:S(2)}, u32[]{:S(2)}) collective-permute-start(bf16[32,2560]{1,0:T(8,128)(2,1)} %get-tuple-element.106), channel_id=1, source_target_pairs={{0,2},{2,4},{4,6},{6,7},{7,5},{5,3},{3,1},{1,0},{8,10},{10,12},{12... | collective-permute-start | bytes 491528 | tf_op jit(solution)/shard_map/cond/branch_0_fun/cond/branch_1_fun/ppermute | solution.py:293
  4.5 7.1 %collective-permute-start.21 = (bf16[32,2560]{1,0:T(8,128)(2,1)}, bf16[32,2560]{1,0:T(8,128)(2,1)}, u32[]{:S(2)}, u32[]{:S(2)}) collective-permute-start(bf16[32,2560]{1,0:T(8,128)(2,1)} %get-tuple-element.107), channel_id=1, source_target_pairs={{0,1},{2,0},{4,2},{6,4},{7,6},{5,7},{3,5},{1,3},{8,9},{10,8},{12,1... | collective-permute-start | bytes 491528 | tf_op jit(solution)/shard_map/cond/branch_0_fun/cond/branch_1_fun/ppermute | solution.py:293
  4.5 10.6 %collective-permute-start.14 = (bf16[32,2560]{1,0:T(8,128)(2,1)}, bf16[32,2560]{1,0:T(8,128)(2,1)}, u32[]{:S(2)}, u32[]{:S(2)}) collective-permute-start(bf16[32,2560]{1,0:T(8,128)(2,1)} %get-tuple-element.106), channel_id=1, source_target_pairs={{0,1},{2,0},{4,2},{6,4},{7,6},{5,7},{3,5},{1,3},{8,9},{10,8},{12,1... | collective-permute-start | bytes 491528 | tf_op jit(solution)/shard_map/cond/branch_0_fun/cond/branch_1_fun/ppermute | solution.py:293
  6.5 8.7 %collective-permute-start.25 = (bf16[32,2560]{1,0:T(8,128)(2,1)}, bf16[32,2560]{1,0:T(8,128)(2,1)}, u32[]{:S(2)}, u32[]{:S(2)}) collective-permute-start(bf16[32,2560]{1,0:T(8,128)(2,1)} %get-tuple-element.107), channel_id=1, source_target_pairs={{0,2},{2,4},{4,6},{6,7},{7,5},{5,3},{3,1},{1,0},{8,10},{10,12},{12... | collective-permute-start | bytes 491528 | tf_op jit(solution)/shard_map/cond/branch_0_fun/cond/branch_1_fun/ppermute | solution.py:293
  8.9 8.3 %collective-permute-start.18 = (bf16[32,2560]{1,0:T(8,128)(2,1)}, bf16[32,2560]{1,0:T(8,128)(2,1)}, u32[]{:S(2)}, u32[]{:S(2)}) collective-permute-start(bf16[32,2560]{1,0:T(8,128)(2,1)} %collective-permute-done.17), channel_id=1, source_target_pairs={{0,2},{2,4},{4,6},{6,7},{7,5},{5,3},{3,1},{1,0},{8,10},{10,12},{12... | collective-permute-start | bytes 491528 | tf_op jit(solution)/shard_map/cond/branch_0_fun/cond/branch_1_fun/ppermute | solution.py:293
  11.6 7.5 %collective-permute-start.22 = (bf16[32,2560]{1,0:T(8,128)(2,1)}, bf16[32,2560]{1,0:T(8,128)(2,1)}, u32[]{:S(2)}, u32[]{:S(2)}) collective-permute-start(bf16[32,2560]{1,0:T(8,128)(2,1)} %collective-permute-done.21), channel_id=1, source_target_pairs={{0,1},{2,0},{4,2},{6,4},{7,6},{5,7},{3,5},{1,3},{8,9},{10,8},{12,1... | collective-permute-start | bytes 491528 | tf_op jit(solution)/shard_map/cond/branch_0_fun/cond/branch_1_fun/ppermute | solution.py:293
  15.1 7.5 %collective-permute-start.15 = (bf16[32,2560]{1,0:T(8,128)(2,1)}, bf16[32,2560]{1,0:T(8,128)(2,1)}, u32[]{:S(2)}, u32[]{:S(2)}) collective-permute-start(bf16[32,2560]{1,0:T(8,128)(2,1)} %collective-permute-done.14), channel_id=1, source_target_pairs={{0,1},{2,0},{4,2},{6,4},{7,6},{5,7},{3,5},{1,3},{8,9},{10,8},{12,1... | collective-permute-start | bytes 491528 | tf_op jit(solution)/shard_map/cond/branch_0_fun/cond/branch_1_fun/ppermute | solution.py:293
  15.1 7.5 %collective-permute-start.26 = (bf16[32,2560]{1,0:T(8,128)(2,1)}, bf16[32,2560]{1,0:T(8,128)(2,1)}, u32[]{:S(2)}, u32[]{:S(2)}) collective-permute-start(bf16[32,2560]{1,0:T(8,128)(2,1)} %collective-permute-done.25), channel_id=1, source_target_pairs={{0,2},{2,4},{4,6},{6,7},{7,5},{5,3},{3,1},{1,0},{8,10},{10,12},{12... | collective-permute-start | bytes 491528 | tf_op jit(solution)/shard_map/cond/branch_0_fun/cond/branch_1_fun/ppermute | solution.py:293
  17.2 8.4 %collective-permute-start.19 = (bf16[32,2560]{1,0:T(8,128)(2,1)}, bf16[32,2560]{1,0:T(8,128)(2,1)}, u32[]{:S(2)}, u32[]{:S(2)}) collective-permute-start(bf16[32,2560]{1,0:T(8,128)(2,1)} %collective-permute-done.18), channel_id=1, source_target_pairs={{0,2},{2,4},{4,6},{6,7},{7,5},{5,3},{3,1},{1,0},{8,10},{10,12},{12... | collective-permute-start | bytes 491528 | tf_op jit(solution)/shard_map/cond/branch_0_fun/cond/branch_1_fun/ppermute | solution.py:293
  19.1 8.2 %collective-permute-start.23 = (bf16[32,2560]{1,0:T(8,128)(2,1)}, bf16[32,2560]{1,0:T(8,128)(2,1)}, u32[]{:S(2)}, u32[]{:S(2)}) collective-permute-start(bf16[32,2560]{1,0:T(8,128)(2,1)} %collective-permute-done.22), channel_id=1, source_target_pairs={{0,1},{2,0},{4,2},{6,4},{7,6},{5,7},{3,5},{1,3},{8,9},{10,8},{12,1... | collective-permute-start | bytes 491528 | tf_op jit(solution)/shard_map/cond/branch_0_fun/cond/branch_1_fun/ppermute | solution.py:293
  22.6 7.2 %collective-permute-start.16 = (bf16[32,2560]{1,0:T(8,128)(2,1)}, bf16[32,2560]{1,0:T(8,128)(2,1)}, u32[]{:S(2)}, u32[]{:S(2)}) collective-permute-start(bf16[32,2560]{1,0:T(8,128)(2,1)} %collective-permute-done.15), channel_id=1, source_target_pairs={{0,1},{2,0},{4,2},{6,4},{7,6},{5,7},{3,5},{1,3},{8,9},{10,8},{12,1... | collective-permute-start | bytes 491528 | tf_op jit(solution)/shard_map/cond/branch_0_fun/cond/branch_1_fun/ppermute | solution.py:293
  22.6 7.4 %collective-permute-start.27 = (bf16[32,2560]{1,0:T(8,128)(2,1)}, bf16[32,2560]{1,0:T(8,128)(2,1)}, u32[]{:S(2)}, u32[]{:S(2)}) collective-permute-start(bf16[32,2560]{1,0:T(8,128)(2,1)} %collective-permute-done.26), channel_id=1, source_target_pairs={{0,2},{2,4},{4,6},{6,7},{7,5},{5,3},{3,1},{1,0},{8,10},{10,12},{12... | collective-permute-start | bytes 491528 | tf_op jit(solution)/shard_map/cond/branch_0_fun/cond/branch_1_fun/ppermute | solution.py:293
  25.6 6.9 %collective-permute-start.20 = (bf16[32,2560]{1,0:T(8,128)(2,1)}, bf16[32,2560]{1,0:T(8,128)(2,1)}, u32[]{:S(2)}, u32[]{:S(2)}) collective-permute-start(bf16[32,2560]{1,0:T(8,128)(2,1)} %collective-permute-done.19), channel_id=1, source_target_pairs={{0,2},{2,4},{4,6},{6,7},{7,5},{5,3},{3,1},{1,0},{8,10},{10,12},{12... | collective-permute-start | bytes 491528 | tf_op jit(solution)/shard_map/cond/branch_0_fun/cond/branch_1_fun/ppermute | solution.py:293
  27.3 5.7 %collective-permute-start.24 = (bf16[32,2560]{1,0:T(8,128)(2,1)}, bf16[32,2560]{1,0:T(8,128)(2,1)}, u32[]{:S(2)}, u32[]{:S(2)}) collective-permute-start(bf16[32,2560]{1,0:T(8,128)(2,1)} %collective-permute-done.23), channel_id=1, source_target_pairs={{0,1},{2,0},{4,2},{6,4},{7,6},{5,7},{3,5},{1,3},{8,9},{10,8},{12,1... | collective-permute-start | bytes 491528 | tf_op jit(solution)/shard_map/cond/branch_0_fun/cond/branch_1_fun/ppermute | solution.py:293
  33.0 9.3 %slice-start.6 = ((s8[4423680]{0:T(1024)(128)(4,1)}), s8[4194304]{0:T(1024)(128)(4,1)S(1)}, s32[]{:S(2)}) async-start(s8[4423680]{0:T(1024)(128)(4,1)} %bitcast.35), calls=%async_computation.6 | async-start | bytes 8388608 | tf_op jit(solution)/shard_map/cond
  33.0 9.3 %slice-start.7 = ((s8[4423680]{0:T(1024)(128)(4,1)}), s8[229376]{0:T(1024)(128)(4,1)S(1)}, s32[]{:S(2)}) async-start(s8[4423680]{0:T(1024)(128)(4,1)} %bitcast.35), calls=%async_computation.7 | async-start | bytes 458752 | tf_op jit(solution)/shard_map/cond
  33.0 9.4 %copy-start.10 = (bf16[32,2560]{1,0:T(8,128)(2,1)S(1)}, bf16[32,2560]{1,0:T(8,128)(2,1)}, u32[]{:S(2)}) copy-start(bf16[32,2560]{1,0:T(8,128)(2,1)} %get-tuple-element.119.refs_0_.rest_1_) | copy-start | bytes 491524 | tf_op jit(solution)/shard_map/cond
  42.3 10.4 %copy-start.5 = (bf16[864,2560]{1,0:T(8,128)(2,1)S(1)}, bf16[864,2560]{1,0:T(8,128)(2,1)}, u32[]{:S(2)}) copy-start(bf16[864,2560]{1,0:T(8,128)(2,1)} %get-tuple-element.135.refs_16_.weight_ref.gate_ref) | copy-start | bytes 13271044 | tf_op jit(solution)/shard_map/cond
  42.3 12.5 %slice-start = ((s8[4423680]{0:T(1024)(128)(4,1)}), s8[4194304]{0:T(1024)(128)(4,1)S(1)}, s32[]{:S(2)}) async-start(s8[4423680]{0:T(1024)(128)(4,1)} %bitcast.25), calls=%async_computation | async-start | bytes 8388608 | tf_op jit(solution)/shard_map/cond
  47.1 59.7 %collective-permute-start.113 = (bf16[896,2816]{1,0:T(8,128)(2,1)}, bf16[896,2816]{1,0:T(8,128)(2,1)}, u32[]{:S(2)}, u32[]{:S(2)}) collective-permute-start(bf16[896,2816]{1,0:T(8,128)(2,1)} %step_rows.8), channel_id=1, source_target_pairs={{0,8},{8,16},{16,24},{24,0},{1,9},{9,17},{17,25},{25,1},{2,10},{10... | collective-permute-start | bytes 15138824 | tf_op jit(solution)/shard_map/cond/branch_0_fun/ppermute | solution.py:290
  52.7 2.1 %slice-start.1 = ((s8[4423680]{0:T(1024)(128)(4,1)}), s8[229376]{0:T(1024)(128)(4,1)S(1)}, s32[]{:S(2)}) async-start(s8[4423680]{0:T(1024)(128)(4,1)} %bitcast.25), calls=%async_computation.1 | async-start | bytes 458752 | tf_op jit(solution)/shard_map/cond
  54.8 4.9 %copy-start.3 = (bf16[720,2560]{1,0:T(8,128)(2,1)}, bf16[720,2560]{1,0:T(8,128)(2,1)S(1)}, u32[]{:S(2)}) copy-start(bf16[720,2560]{1,0:T(8,128)(2,1)S(1)} %step_rows.7.rest_0_.refs_0_) | copy-start | bytes 11059204 | tf_op jit(solution)/shard_map/cond
  59.9 7.5 %collective-permute-start.105 = (bf16[32,2560]{1,0:T(8,128)(2,1)S(1)}, bf16[32,2560]{1,0:T(8,128)(2,1)S(1)}, u32[]{:S(2)}, u32[]{:S(2)}) collective-permute-start(bf16[32,2560]{1,0:T(8,128)(2,1)S(1)} %get-tuple-element.245), channel_id=1, source_target_pairs={{0,2},{2,4},{4,6},{6,7},{7,5},{5,3},{3,1},{1,0},{8,10},{10,12},{12... | collective-permute-start | bytes 491528 | tf_op jit(solution)/shard_map/cond/branch_0_fun/cond/branch_1_fun/ppermute | solution.py:293
  62.4 10.7 %collective-permute-start.108 = (bf16[32,2560]{1,0:T(8,128)(2,1)S(1)}, bf16[32,2560]{1,0:T(8,128)(2,1)S(1)}, u32[]{:S(2)}, u32[]{:S(2)}) collective-permute-start(bf16[32,2560]{1,0:T(8,128)(2,1)S(1)} %get-tuple-element.246), channel_id=1, source_target_pairs={{0,1},{2,0},{4,2},{6,4},{7,6},{5,7},{3,5},{1,3},{8,9},{10,8},{12,1... | collective-permute-start | bytes 491528 | tf_op jit(solution)/shard_map/cond/branch_0_fun/cond/branch_1_fun/ppermute | solution.py:293
  62.6 8.4 %collective-permute-start.98 = (bf16[32,2560]{1,0:T(8,128)(2,1)S(1)}, bf16[32,2560]{1,0:T(8,128)(2,1)S(1)}, u32[]{:S(2)}, u32[]{:S(2)}) collective-permute-start(bf16[32,2560]{1,0:T(8,128)(2,1)S(1)} %get-tuple-element.247), channel_id=1, source_target_pairs={{0,2},{2,4},{4,6},{6,7},{7,5},{5,3},{3,1},{1,0},{8,10},{10,12},{12... | collective-permute-start | bytes 491528 | tf_op jit(solution)/shard_map/cond/branch_0_fun/cond/branch_1_fun/ppermute | solution.py:293
  64.6 18.7 %collective-permute-start.102 = (bf16[32,2560]{1,0:T(8,128)(2,1)S(1)}, bf16[32,2560]{1,0:T(8,128)(2,1)S(1)}, u32[]{:S(2)}, u32[]{:S(2)}) collective-permute-start(bf16[32,2560]{1,0:T(8,128)(2,1)S(1)} %get-tuple-element.248), channel_id=1, source_target_pairs={{0,1},{2,0},{4,2},{6,4},{7,6},{5,7},{3,5},{1,3},{8,9},{10,8},{12,1... | collective-permute-start | bytes 491528 | tf_op jit(solution)/shard_map/cond/branch_0_fun/cond/branch_1_fun/ppermute | solution.py:293
  67.5 7.2 %collective-permute-start.106 = (bf16[32,2560]{1,0:T(8,128)(2,1)S(1)}, bf16[32,2560]{1,0:T(8,128)(2,1)S(1)}, u32[]{:S(2)}, u32[]{:S(2)}) collective-permute-start(bf16[32,2560]{1,0:T(8,128)(2,1)S(1)} %add_convert_fusion.17), channel_id=1, source_target_pairs={{0,2},{2,4},{4,6},{6,7},{7,5},{5,3},{3,1},{1,0},{8,10},{10,12},{12... | collective-permute-start | bytes 491528 | tf_op jit(solution)/shard_map/cond/branch_0_fun/cond/branch_1_fun/ppermute | solution.py:293
  71.0 6.8 %collective-permute-start.99 = (bf16[32,2560]{1,0:T(8,128)(2,1)S(1)}, bf16[32,2560]{1,0:T(8,128)(2,1)S(1)}, u32[]{:S(2)}, u32[]{:S(2)}) collective-permute-start(bf16[32,2560]{1,0:T(8,128)(2,1)S(1)} %add_convert_fusion.23), channel_id=1, source_target_pairs={{0,2},{2,4},{4,6},{6,7},{7,5},{5,3},{3,1},{1,0},{8,10},{10,12},{12... | collective-permute-start | bytes 491528 | tf_op jit(solution)/shard_map/cond/branch_0_fun/cond/branch_1_fun/ppermute | solution.py:293
  74.7 6.5 %collective-permute-start.109 = (bf16[32,2560]{1,0:T(8,128)(2,1)S(1)}, bf16[32,2560]{1,0:T(8,128)(2,1)S(1)}, u32[]{:S(2)}, u32[]{:S(2)}) collective-permute-start(bf16[32,2560]{1,0:T(8,128)(2,1)S(1)} %get-tuple-element.242), channel_id=1, source_target_pairs={{0,1},{2,0},{4,2},{6,4},{7,6},{5,7},{3,5},{1,3},{8,9},{10,8},{12,1... | collective-permute-start | bytes 491528 | tf_op jit(solution)/shard_map/cond/branch_0_fun/cond/branch_1_fun/ppermute | solution.py:293
  76.4 17.5 %collective-permute-start.107 = (bf16[32,2560]{1,0:T(8,128)(2,1)S(1)}, bf16[32,2560]{1,0:T(8,128)(2,1)S(1)}, u32[]{:S(2)}, u32[]{:S(2)}) collective-permute-start(bf16[32,2560]{1,0:T(8,128)(2,1)S(1)} %get-tuple-element.241), channel_id=1, source_target_pairs={{0,2},{2,4},{4,6},{6,7},{7,5},{5,3},{3,1},{1,0},{8,10},{10,12},{12... | collective-permute-start | bytes 491528 | tf_op jit(solution)/shard_map/cond/branch_0_fun/cond/branch_1_fun/ppermute | solution.py:293
  77.8 5.8 %collective-permute-start.100 = (bf16[32,2560]{1,0:T(8,128)(2,1)S(1)}, bf16[32,2560]{1,0:T(8,128)(2,1)S(1)}, u32[]{:S(2)}, u32[]{:S(2)}) collective-permute-start(bf16[32,2560]{1,0:T(8,128)(2,1)S(1)} %add_convert_fusion.22), channel_id=1, source_target_pairs={{0,2},{2,4},{4,6},{6,7},{7,5},{5,3},{3,1},{1,0},{8,10},{10,12},{12... | collective-permute-start | bytes 491528 | tf_op jit(solution)/shard_map/cond/branch_0_fun/cond/branch_1_fun/ppermute | solution.py:293
  81.3 7.6 %collective-permute-start.110 = (bf16[32,2560]{1,0:T(8,128)(2,1)S(1)}, bf16[32,2560]{1,0:T(8,128)(2,1)S(1)}, u32[]{:S(2)}, u32[]{:S(2)}) collective-permute-start(bf16[32,2560]{1,0:T(8,128)(2,1)S(1)} %add_convert_fusion.14), channel_id=1, source_target_pairs={{0,1},{2,0},{4,2},{6,4},{7,6},{5,7},{3,5},{1,3},{8,9},{10,8},{12,1... | collective-permute-start | bytes 491528 | tf_op jit(solution)/shard_map/cond/branch_0_fun/cond/branch_1_fun/ppermute | solution.py:293
  83.6 8.7 %collective-permute-start.103 = (bf16[32,2560]{1,0:T(8,128)(2,1)S(1)}, bf16[32,2560]{1,0:T(8,128)(2,1)S(1)}, u32[]{:S(2)}, u32[]{:S(2)}) collective-permute-start(bf16[32,2560]{1,0:T(8,128)(2,1)S(1)} %get-tuple-element.244), channel_id=1, source_target_pairs={{0,1},{2,0},{4,2},{6,4},{7,6},{5,7},{3,5},{1,3},{8,9},{10,8},{12,1... | collective-permute-start | bytes 491528 | tf_op jit(solution)/shard_map/cond/branch_0_fun/cond/branch_1_fun/ppermute | solution.py:293
  85.5 9.1 %collective-permute-start.101 = (bf16[32,2560]{1,0:T(8,128)(2,1)S(1)}, bf16[32,2560]{1,0:T(8,128)(2,1)S(1)}, u32[]{:S(2)}, u32[]{:S(2)}) collective-permute-start(bf16[32,2560]{1,0:T(8,128)(2,1)S(1)} %get-tuple-element.243), channel_id=1, source_target_pairs={{0,2},{2,4},{4,6},{6,7},{7,5},{5,3},{3,1},{1,0},{8,10},{10,12},{12... | collective-permute-start | bytes 491528 | tf_op jit(solution)/shard_map/cond/branch_0_fun/cond/branch_1_fun/ppermute | solution.py:293
  88.9 5.7 %collective-permute-start.111 = (bf16[32,2560]{1,0:T(8,128)(2,1)S(1)}, bf16[32,2560]{1,0:T(8,128)(2,1)S(1)}, u32[]{:S(2)}, u32[]{:S(2)}) collective-permute-start(bf16[32,2560]{1,0:T(8,128)(2,1)S(1)} %add_convert_fusion.13), channel_id=1, source_target_pairs={{0,1},{2,0},{4,2},{6,4},{7,6},{5,7},{3,5},{1,3},{8,9},{10,8},{12,1... | collective-permute-start | bytes 491528 | tf_op jit(solution)/shard_map/cond/branch_0_fun/cond/branch_1_fun/ppermute | solution.py:293
  92.4 5.4 %collective-permute-start.104 = (bf16[32,2560]{1,0:T(8,128)(2,1)S(1)}, bf16[32,2560]{1,0:T(8,128)(2,1)S(1)}, u32[]{:S(2)}, u32[]{:S(2)}) collective-permute-start(bf16[32,2560]{1,0:T(8,128)(2,1)S(1)} %add_convert_fusion.19), channel_id=1, source_target_pairs={{0,1},{2,0},{4,2},{6,4},{7,6},{5,7},{3,5},{1,3},{8,9},{10,8},{12,1... | collective-permute-start | bytes 491528 | tf_op jit(solution)/shard_map/cond/branch_0_fun/cond/branch_1_fun/ppermute | solution.py:293
  98.0 11.3 %copy-start.16 = (bf16[32,2560]{1,0:T(8,128)(2,1)}, bf16[32,2560]{1,0:T(8,128)(2,1)S(1)}, u32[]{:S(2)}) copy-start(bf16[32,2560]{1,0:T(8,128)(2,1)S(1)} %get-tuple-element.362) | copy-start | bytes 491524 | tf_op jit(solution)/shard_map/cond
  98.0 49.6 %collective-permute-start.115 = (bf16[720,2560]{1,0:T(8,128)(2,1)}, bf16[720,2560]{1,0:T(8,128)(2,1)}, u32[]{:S(2)}, u32[]{:S(2)}) collective-permute-start(bf16[720,2560]{1,0:T(8,128)(2,1)} %copy-done.3), channel_id=1, source_target_pairs={{0,8},{8,16},{16,24},{24,0},{1,9},{9,17},{17,25},{25,1},{2,10},{10... | collective-permute-start | bytes 11059208 | tf_op jit(solution)/shard_map/cond/branch_0_fun/ppermute | solution.py:290
  108.3 45.8 %collective-permute-start.114 = (bf16[144,2560]{1,0:T(8,128)(2,1)S(1)}, bf16[144,2560]{1,0:T(8,128)(2,1)S(1)}, u32[]{:S(2)}, u32[]{:S(2)}) collective-permute-start(bf16[144,2560]{1,0:T(8,128)(2,1)S(1)} %step_rows.9.refs_13_.refs_0_), channel_id=1, source_target_pairs={{0,8},{8,16},{16,24},{24,0},{1,9},{9,17},{17,25},{25,1},{2,10},{10... | collective-permute-start | bytes 2211848 | tf_op jit(solution)/shard_map/cond/branch_0_fun/ppermute | solution.py:290
  109.4 6.5 %collective-permute-start.38 = (bf16[32,2560]{1,0:T(8,128)(2,1)S(1)}, bf16[32,2560]{1,0:T(8,128)(2,1)}, u32[]{:S(2)}, u32[]{:S(2)}) collective-permute-start(bf16[32,2560]{1,0:T(8,128)(2,1)S(1)} %get-tuple-element.115), channel_id=1, source_target_pairs={{0,2},{2,4},{4,6},{6,7},{7,5},{5,3},{3,1},{1,0},{8,10},{10,12},{12... | collective-permute-start | bytes 491528 | tf_op jit(solution)/shard_map/cond/branch_0_fun/cond/branch_1_fun/ppermute | solution.py:293
  111.8 6.8 %collective-permute-start.35 = (bf16[32,2560]{1,0:T(8,128)(2,1)S(1)}, bf16[32,2560]{1,0:T(8,128)(2,1)}, u32[]{:S(2)}, u32[]{:S(2)}) collective-permute-start(bf16[32,2560]{1,0:T(8,128)(2,1)S(1)} %get-tuple-element.115), channel_id=1, source_target_pairs={{0,1},{2,0},{4,2},{6,4},{7,6},{5,7},{3,5},{1,3},{8,9},{10,8},{12,1... | collective-permute-start | bytes 491528 | tf_op jit(solution)/shard_map/cond/branch_0_fun/cond/branch_1_fun/ppermute | solution.py:293
  115.8 7.9 %collective-permute-start.39 = (bf16[32,2560]{1,0:T(8,128)(2,1)}, bf16[32,2560]{1,0:T(8,128)(2,1)}, u32[]{:S(2)}, u32[]{:S(2)}) collective-permute-start(bf16[32,2560]{1,0:T(8,128)(2,1)} %collective-permute-done.38), channel_id=1, source_target_pairs={{0,2},{2,4},{4,6},{6,7},{7,5},{5,3},{3,1},{1,0},{8,10},{10,12},{12... | collective-permute-start | bytes 491528 | tf_op jit(solution)/shard_map/cond/branch_0_fun/cond/branch_1_fun/ppermute | solution.py:293
  118.7 6.9 %collective-permute-start.36 = (bf16[32,2560]{1,0:T(8,128)(2,1)}, bf16[32,2560]{1,0:T(8,128)(2,1)}, u32[]{:S(2)}, u32[]{:S(2)}) collective-permute-start(bf16[32,2560]{1,0:T(8,128)(2,1)} %collective-permute-done.35), channel_id=1, source_target_pairs={{0,1},{2,0},{4,2},{6,4},{7,6},{5,7},{3,5},{1,3},{8,9},{10,8},{12,1... | collective-permute-start | bytes 491528 | tf_op jit(solution)/shard_map/cond/branch_0_fun/cond/branch_1_fun/ppermute | solution.py:293
  123.7 6.5 %collective-permute-start.40 = (bf16[32,2560]{1,0:T(8,128)(2,1)}, bf16[32,2560]{1,0:T(8,128)(2,1)}, u32[]{:S(2)}, u32[]{:S(2)}) collective-permute-start(bf16[32,2560]{1,0:T(8,128)(2,1)} %collective-permute-done.39), channel_id=1, source_target_pairs={{0,2},{2,4},{4,6},{6,7},{7,5},{5,3},{3,1},{1,0},{8,10},{10,12},{12... | collective-permute-start | bytes 491528 | tf_op jit(solution)/shard_map/cond/branch_0_fun/cond/branch_1_fun/ppermute | solution.py:293
  125.5 13.4 %collective-permute-start.37 = (bf16[32,2560]{1,0:T(8,128)(2,1)}, bf16[32,2560]{1,0:T(8,128)(2,1)}, u32[]{:S(2)}, u32[]{:S(2)}) collective-permute-start(bf16[32,2560]{1,0:T(8,128)(2,1)} %collective-permute-done.36), channel_id=1, source_target_pairs={{0,1},{2,0},{4,2},{6,4},{7,6},{5,7},{3,5},{1,3},{8,9},{10,8},{12,1... | collective-permute-start | bytes 491528 | tf_op jit(solution)/shard_map/cond/branch_0_fun/cond/branch_1_fun/ppermute | solution.py:293
  130.2 8.7 %collective-permute-start.41 = (bf16[32,2560]{1,0:T(8,128)(2,1)}, bf16[32,2560]{1,0:T(8,128)(2,1)}, u32[]{:S(2)}, u32[]{:S(2)}) collective-permute-start(bf16[32,2560]{1,0:T(8,128)(2,1)} %collective-permute-done.40), channel_id=1, source_target_pairs={{0,2},{2,4},{4,6},{6,7},{7,5},{5,3},{3,1},{1,0},{8,10},{10,12},{12... | collective-permute-start | bytes 491528 | tf_op jit(solution)/shard_map/cond/branch_0_fun/cond/branch_1_fun/ppermute | solution.py:293
  139.0 8.7 %copy-start.4 = (bf16[720,2560]{1,0:T(8,128)(2,1)S(1)}, bf16[720,2560]{1,0:T(8,128)(2,1)}, u32[]{:S(2)}) copy-start(bf16[720,2560]{1,0:T(8,128)(2,1)} %copy-done.3) | copy-start | bytes 11059204 | tf_op jit(solution)/shard_map/cond
  147.6 6.2 %copy-start.7 = (bf16[864,2560]{1,0:T(8,128)(2,1)}, bf16[864,2560]{1,0:T(8,128)(2,1)S(1)}, u32[]{:S(2)}) copy-start(bf16[864,2560]{1,0:T(8,128)(2,1)S(1)} %mean_of_steps.2.refs_2_) | copy-start | bytes 13271044 | tf_op jit(solution)/shard_map/cond
  155.2 0.7 copy-start.14
